TPU v7x, 32 devices: a whole 2x2x4 slice. The times are simulated.
32 devices in a mesh: groups: 2 (over y), adapt: 16 (over z, x, core).
Axes of the slice: x: 2, y: 2, z: 4, core: 2. Of those that a mesh axis runs over, the one named last changes fastest.
Arguments:
- hidden: bfloat16 [2048, 8192], P(('groups', 'adapt')), parts along dimension 0, may hold values from -6 to 6
- frozen_query: bfloat16 [2048, 8192], P(('groups', 'adapt')), parts along dimension 0, may hold values from -30 to 30
- keys: bfloat16 [32, 1088, 1024], P(('groups', 'adapt')), parts along dimension 0, may hold values from -24 to 24
- values: bfloat16 [32, 1088, 1024], P(('groups', 'adapt')), parts along dimension 0, may hold values from -6 to 6
- cache_length: int32 [32], P(('groups', 'adapt')), parts along dimension 0, may hold values from 1 to 1024, 8192 in all
- adapter_index: int32 [2048, 2], P(('groups', 'adapt')), parts along dimension 0, may hold values from 0 to 127, all different within a row; in each aligned block of 64 rows (0 to 63, 64 to 127, ...) at most 2 rows name the same one
- adapter_down_weight: bfloat16 [256, 32, 8192], P(('groups', 'adapt')), parts along dimension 0, may hold values from -0.0625 to 0.0625
- adapter_up_weight: bfloat16 [256, 32, 8192], P(('groups', 'adapt')), parts along dimension 0, may hold values from -1 to 1
Outputs:
- context: bfloat16 [2048, 2, 8192], P(('groups', 'adapt')), parts along dimension 0
There are 2 independent parts, one for each index of `groups`. A program takes and returns all parts, laid end to end along the dimension named above; each array names one. Nothing has to cross between parts.
Inputs may be any that keep to these rules, and one draw needn't show every extreme that they name: `adapter_index`: among the 64 tokens of one device (with 2 ids each), no adapter is named more than 2 times, a bound that some block reaches; the 2 ids of a token differ. `cache_length`: within each part the live slots of the 16 prompts sum to 8192.
All inputs are finite; a program needn't handle non-finite values. No bound on the sum of `cache_length` on one device may be relied on, other than what follows from the above.
Results may differ from a plain program's by a relative error of at most 0.0083.
Values may be sent and summed in bfloat16 or wider, within the bound.
A program may use at most 192 MiB of HBM per device.

v0:
```python
import math

import jax
import jax.numpy as jnp
from jax import lax
from jax.sharding import PartitionSpec as P

HEAD = 128
CAP = 2


ADAPTER_SCALE = 0.5


def attend(adapted_query_rows, key_block, value_block, cached):
    tok_rows, per_token, model_width = adapted_query_rows.shape
    key_total, kv_width = key_block.shape
    kv_heads = kv_width // HEAD
    group_size = model_width // kv_width
    split_query = adapted_query_rows.reshape(tok_rows, per_token, kv_heads, group_size, HEAD)
    split_keys = key_block.reshape(key_total, kv_heads, HEAD)
    split_values = value_block.reshape(key_total, kv_heads, HEAD)
    scores = jnp.einsum(
        "tagqe,jge->tagqj", split_query, split_keys, preferred_element_type=jnp.float32
    ) * (1.0 / math.sqrt(HEAD))
    key_index = lax.broadcasted_iota(jnp.int32, (tok_rows, key_total), 1)
    tok_index = lax.broadcasted_iota(jnp.int32, (tok_rows, key_total), 0)
    history = key_total - tok_rows
    visible = (key_index >= history - cached) & (key_index <= history + tok_index)
    visible = visible[:, None, None, None, :]
    scores = jnp.where(visible, scores, -1e30)
    row_peak = jnp.max(scores, axis=-1, keepdims=True)
    raised = jnp.where(visible, jnp.exp(scores - row_peak), 0.0)
    weights = (raised / jnp.sum(raised, axis=-1, keepdims=True)).astype(jnp.bfloat16)
    mixed_rows = jnp.einsum(
        "tagqj,jge->tagqe", weights, split_values, preferred_element_type=jnp.float32
    )
    return mixed_rows.reshape(tok_rows, per_token, model_width).astype(jnp.bfloat16)


def body(
    hidden,
    frozen_query,
    keys,
    values,
    cache_length,
    adapter_index,
    adapter_down_weight,
    adapter_up_weight,
):
    tok_rows, model_width = hidden.shape
    per_token = adapter_index.shape[1]
    resident_count = adapter_down_weight.shape[0]
    owners = lax.axis_size("adapt")
    flat_ids = adapter_index.reshape(-1)
    row_total = flat_ids.shape[0]
    row_index = lax.broadcasted_iota(jnp.int32, (row_total, row_total), 0)
    col_index = lax.broadcasted_iota(jnp.int32, (row_total, row_total), 1)
    matches = (flat_ids[:, None] == flat_ids[None, :]) & (col_index < row_index)
    rank_in = jnp.sum(matches.astype(jnp.int32), axis=1)
    position = flat_ids * CAP + rank_in
    sources = jnp.broadcast_to(hidden[:, None, :], (tok_rows, per_token, model_width)).reshape(
        row_total, model_width
    )
    outgoing = (
        jnp.zeros((owners * resident_count * CAP, model_width), jnp.bfloat16)
        .at[position]
        .set(sources)
    )
    outgoing = outgoing.reshape(owners, resident_count, CAP, model_width)
    reduced_rows = jnp.einsum(
        "qtue,tve->qtuv",
        lax.all_to_all(outgoing, "adapt", split_axis=0, concat_axis=0, tiled=True),
        adapter_down_weight,
        preferred_element_type=jnp.float32,
    ).astype(jnp.bfloat16)
    returned = lax.all_to_all(
        jnp.einsum(
            "afok,fkx->afox", reduced_rows, adapter_up_weight, preferred_element_type=jnp.float32
        ).astype(jnp.bfloat16),
        "adapt",
        split_axis=0,
        concat_axis=0,
        tiled=True,
    )
    update_rows = returned.reshape(owners * resident_count * CAP, model_width)[position]
    update_rows = update_rows.reshape(tok_rows, per_token, model_width)
    adapted_query_rows = (
        frozen_query[:, None, :].astype(jnp.float32)
        + ADAPTER_SCALE * update_rows.astype(jnp.float32)
    ).astype(jnp.bfloat16)
    return attend(adapted_query_rows, keys[0], values[0], cache_length[0])


def solution(mesh):
    in_specs = (
        P(("groups", "adapt"), None),
        P(("groups", "adapt"), None),
        P(("groups", "adapt"), None, None),
        P(("groups", "adapt"), None, None),
        P(("groups", "adapt")),
        P(("groups", "adapt"), None),
        P(("groups", "adapt"), None, None),
        P(("groups", "adapt"), None, None),
    )
    out_specs = P(("groups", "adapt"), None, None)
    return jax.shard_map(body, mesh=mesh, in_specs=in_specs, out_specs=out_specs, check_vma=False)
```

profile of v0, /device:TPU:15, one launch (start us, length us, event | category | flops | bytes accessed | tf_op | source)
XLA Modules:
  0.0 296.1 jit_solution(11932920446240554548)
XLA Ops:
  0.0 0.7 broadcast_multiply_fusion
  0.7 0.8 copy.55
  1.4 0.1 copy.54
  1.5 0.1 mul.35
  1.7 0.1 eq.15
  1.8 0.2 convert_reduce_fusion
  2.0 3.3 %broadcast_in_dim.38 = bf16[64,2,8192]{2,1,0:T(2,128)(2,1)S(1)} broadcast(bf16[64,8192]{1,0:T(8,128)(2,1)} %param.8), dimensions={0,2} | broadcast | bytes 3145728 | tf_op jit(solution)/shard_map/broadcast_in_dim | solution.py:62
  5.3 2.2 reshape.99
  7.5 7.0 %scatter_custom_fusion = bf16[256,8192]{1,0:T(8,128)(2,1)} fusion(s32[128]{0:T(128)S(1)} %fusion.46, bf16[128,8192]{1,0:T(8,128)(2,1)} %reshape.99, bf16[]{:T(256)} %constant.2.clone.1), kind=kCustom, calls=%fused_computation.27 | custom fusion | bytes 4194816 | tf_op jit(solution)/shard_map/scatter | solution.py:68
  14.5 7.6 %reshape.84 = bf16[16,8,2,8192]{3,2,1,0:T(2,128)(2,1)} reshape(bf16[256,8192]{1,0:T(8,128)(2,1)} %scatter_custom_fusion) | data formatting | bytes 8388608 | tf_op jit(solution)/shard_map/reshape | solution.py:70
  22.1 98.9 %all_to_all.10 = bf16[16,8,2,8192]{3,2,1,0:T(2,128)(2,1)} all-to-all(bf16[16,8,2,8192]{3,2,1,0:T(2,128)(2,1)} %reshape.84), channel_id=1, replica_groups=mesh['groups'=2,'adapt'=16] {'adapt'}, dimensions={0} | all-to-all | bytes 8388608 | tf_op jit(solution)/shard_map/all_to_all | solution.py:73
  121.0 10.5 %fusion.10 = bf16[16,8,2,8192]{3,0,2,1:T(8,128)(2,1)} fusion(bf16[8,32,8192]{2,1,0:T(8,128)(2,1)} %param.15, bf16[8,32,8192]{2,1,0:T(8,128)(2,1)} %param.14, bf16[16,8,2,8192]{3,2,1,0:T(2,128)(2,1)} %all_to_all.10), kind=kOutput, calls=%fused_computation.15 | convolution fusion | flops 270540800 | bytes 16777216 | tf_op jit(solution)/shard_map/afok,fkx->afox/dot_general | solution.py:78
  131.5 8.5 %copy.57 = bf16[16,8,2,8192]{3,2,1,0:T(2,128)(2,1)} copy(bf16[16,8,2,8192]{3,0,2,1:T(8,128)(2,1)} %fusion.10) | data formatting | bytes 8388608 | tf_op jit(solution)/shard_map/convert_element_type | solution.py:80
  140.1 5.5 %all-to-all-start.1 = ((bf16[16,8,2,8192]{3,2,1,0:T(2,128)(2,1)}), bf16[16,8,2,8192]{3,2,1,0:T(2,128)(2,1)}, u32[]{:S(2)}, u32[]{:S(2)}) async-start(bf16[16,8,2,8192]{3,2,1,0:T(2,128)(2,1)} %copy.57), calls=%async_computation.1 | async-start | bytes 8388608 | tf_op jit(solution)/shard_map/all_to_all | solution.py:77
  145.5 0.0 copy-done.3
  145.5 0.0 copy-start
  145.5 0.1 convert_bitcast_fusion
  145.7 0.0 copy-start.1
  145.7 1.7 copy.73
  147.4 0.1 copy-done
  147.4 2.0 copy.75
  150.1 2.0 copy.76
  152.1 0.1 fusion.44
  152.3 85.7 %all-to-all-done.1 = bf16[16,8,2,8192]{3,2,1,0:T(2,128)(2,1)} async-done(((bf16[16,8,2,8192]{3,2,1,0:T(2,128)(2,1)}), bf16[16,8,2,8192]{3,2,1,0:T(2,128)(2,1)}, u32[]{:S(2)}, u32[]{:S(2)}) %all-to-all-start.1) | async-done | bytes 4194336 | tf_op jit(solution)/shard_map/all_to_all | solution.py:77
  238.0 7.2 %reshape.85 = bf16[256,8192]{1,0:T(8,128)(2,1)} reshape(bf16[16,8,2,8192]{3,2,1,0:T(2,128)(2,1)} %all-to-all-done.1) | data formatting | bytes 8388608 | tf_op jit(solution)/shard_map/reshape | solution.py:86
  245.2 6.5 %gather_fusion = bf16[128,8192]{1,0:T(8,128)(2,1)S(1)} fusion(bf16[256,8192]{1,0:T(8,128)(2,1)} %reshape.85, s32[1024]{0:T(1024)S(1)} %pad_clamp_fusion), kind=kCustom, calls=%fused_computation | custom fusion | bytes 4194816 | tf_op jit(solution)/shard_map/gather | solution.py:86
  251.7 0.4 multiply_bitcast_fusion
  252.1 2.7 copy.74
  254.8 24.6 %fusion.53 = (f32[64,2,8,8]{3,1,0,2:T(2,128)S(1)}, f32[64,2,8,8,1088]{4,3,1,0,2:T(8,128)}) fusion(pred[64,1088]{1,0:T(8,128)(4,1)S(1)} %fusion.44, bf16[1088,8,128,1,1]{2,1,0,4,3:T(8,128)(2,1)} %bitcast.68, f32[64,2,8,8,128]{4,3,2,1,0:T(8,128)} %bitcast.64, f32[64,8,8,128]{3,2,1,0:T(8,128)} %bitcast.69), kind=kOutput, calls=%fused_computation.48 | convolution fusion | flops 2328364032 | bytes 44273664 | tf_op jit(solution)/shard_map/sub | solution.py:33
  279.5 14.0 %convert_bitcast_fusion.1 = bf16[64,2,8,8,128]{4,3,1,0,2:T(8,128)(2,1)S(1)} fusion(bf16[1088,8,128,1,1]{2,1,0,4,3:T(8,128)(2,1)S(1)} %bitcast.67, f32[64,2,8,8,1088]{4,3,1,0,2:T(8,128)} %get-tuple-element.6, f32[64,2,8,8]{3,1,0,2:T(2,128)S(1)} %get-tuple-element.5), kind=kOutput, calls=%fused_computation.26 | convolution fusion | flops 2300575744 | bytes 40009728 | tf_op jit(solution)/shard_map/tagqj,jge->tagqe/dot_general | solution.py:35
  293.5 0.6 copy.71
  294.1 2.0 reshape.107
  (8 shorter events, 0.0 us)
Async XLA Ops:
  140.1 5.5 %copy-start.3 = (bf16[64,8192]{1,0:T(8,128)(2,1)S(1)}, bf16[64,8192]{1,0:T(8,128)(2,1)}, u32[]{:S(2)}) copy-start(bf16[64,8192]{1,0:T(8,128)(2,1)} %param.9) | copy-start | bytes 3145732
  140.1 97.9 %all-to-all-start.1 = ((bf16[16,8,2,8192]{3,2,1,0:T(2,128)(2,1)}), bf16[16,8,2,8192]{3,2,1,0:T(2,128)(2,1)}, u32[]{:S(2)}, u32[]{:S(2)}) async-start(bf16[16,8,2,8192]{3,2,1,0:T(2,128)(2,1)} %copy.57), calls=%async_computation.1 | async-start | bytes 8388608 | tf_op jit(solution)/shard_map/all_to_all | solution.py:77
  145.5 1.9 copy-start
  145.7 4.4 %copy-start.1 = (bf16[1,1088,1024]{2,1,0:T(8,128)(2,1)S(1)}, bf16[1,1088,1024]{2,1,0:T(8,128)(2,1)}, u32[]{:S(2)}) copy-start(bf16[1,1088,1024]{2,1,0:T(8,128)(2,1)} %param.11) | copy-start | bytes 6684676
  254.8 24.7 %copy-start.2 = (bf16[136,8,8,128]{3,2,1,0:T(8,128)(2,1)S(1)}, bf16[136,8,8,128]{3,2,1,0:T(8,128)(2,1)}, u32[]{:S(2)}) copy-start(bf16[136,8,8,128]{3,2,1,0:T(8,128)(2,1)} %copy.76) | copy-start | bytes 6684676
where the time goes:
time: 297 us; the launch traced here: 296 us
  blocking collectives  98.9 us (33%)
  waiting for transfers between devices  85.7 us (29%)
  local copies, waits for them, and re-layouts  54.5 us (18%)
  matrix products  49.1 us (17%)
  starting transfers between devices  5.46 us (2%)
    all_to_all x1, blocking collectives, body(): lax.all_to_all(outgoing, 'adapt', split_axis=0, concat_axis=0, tiled=True)  98.9 us
    all_to_all x1, waiting for transfers between devices, body(): lax.all_to_all(jnp.einsum('afok,fkx->afox', reduced_rows, adapter_up_weig...  85.7 us
    sub x1, matrix products, attend(): raised = jnp.where(visible, jnp.exp(scores - row_peak), 0.0)  24.6 us
    dot_general x1, matrix products, attend(): jnp.einsum('tagqj,jge->tagqe', weights, split_values, preferred_element_t...  14 us
    dot_general x1, matrix products, body(): jnp.einsum('afok,fkx->afox', reduced_rows, adapter_up_weight, preferred_e...  10.5 us
    unnamed x13, local copies, waits for them, and re-layouts  9.23 us
    convert_element_type x1, local copies, waits for them, and re-layouts, body(): returned = lax.all_to_all(jnp.einsum('afok,fkx->afox', reduced_rows, adap...  8.52 us
    reshape x1, local copies, waits for them, and re-layouts, body(): outgoing = outgoing.reshape(owners, resident_count, CAP, model_width)  7.62 us
  transfers between devices with their start and end apart: 1, of which 1 were waited for; matrix products, arithmetic and copies ran while one was open for 2% of the time, Pallas kernels for 0%

commit v1 on v0

v1 whole, which is shorter than its diff:
```python
import functools
import math

import jax
import jax.numpy as jnp
from jax import lax
from jax.experimental import pallas as pl
from jax.experimental.pallas import tpu as pltpu
from jax.sharding import PartitionSpec as P

HEAD = 128
CAP = 2
ADAPTER_SCALE = 0.5
VMEM_LIMIT = 56 * 1024 * 1024


def attend_all(adapted_query_rows, key_block, value_block, cached):
    tok_rows, per_token, model_width = adapted_query_rows.shape
    key_total, kv_width = key_block.shape
    kv_heads = kv_width // HEAD
    group_size = model_width // kv_width
    split_query = adapted_query_rows.reshape(tok_rows, per_token, kv_heads, group_size, HEAD)
    split_keys = key_block.reshape(key_total, kv_heads, HEAD)
    split_values = value_block.reshape(key_total, kv_heads, HEAD)
    scores = jnp.einsum(
        "tagqe,jge->tagqj", split_query, split_keys, preferred_element_type=jnp.float32
    ) * (1.0 / math.sqrt(HEAD))
    key_index = lax.broadcasted_iota(jnp.int32, (tok_rows, key_total), 1)
    tok_index = lax.broadcasted_iota(jnp.int32, (tok_rows, key_total), 0)
    history = key_total - tok_rows
    visible = (key_index >= history - cached) & (key_index <= history + tok_index)
    visible = visible[:, None, None, None, :]
    scores = jnp.where(visible, scores, -1e30)
    row_peak = jnp.max(scores, axis=-1, keepdims=True)
    raised = jnp.where(visible, jnp.exp(scores - row_peak), 0.0)
    weights = (raised / jnp.sum(raised, axis=-1, keepdims=True)).astype(jnp.bfloat16)
    mixed_rows = jnp.einsum(
        "tagqj,jge->tagqe", weights, split_values, preferred_element_type=jnp.float32
    )
    return mixed_rows.reshape(tok_rows, per_token, model_width).astype(jnp.bfloat16)


def full_slots(hidden, frozen_query, keys, values, cache_length, adapter_index, down, up):
    tok_rows, model_width = hidden.shape
    per_token = adapter_index.shape[1]
    resident_count = down.shape[0]
    owners = lax.axis_size("adapt")
    flat_ids = adapter_index.reshape(-1)
    row_total = flat_ids.shape[0]
    row_index = lax.broadcasted_iota(jnp.int32, (row_total, row_total), 0)
    col_index = lax.broadcasted_iota(jnp.int32, (row_total, row_total), 1)
    matches = (flat_ids[:, None] == flat_ids[None, :]) & (col_index < row_index)
    position = flat_ids * CAP + jnp.sum(matches.astype(jnp.int32), axis=1)
    sources = jnp.broadcast_to(hidden[:, None, :], (tok_rows, per_token, model_width)).reshape(
        row_total, model_width
    )
    outgoing = (
        jnp.zeros((owners * resident_count * CAP, model_width), jnp.bfloat16)
        .at[position]
        .set(sources)
    )
    outgoing = outgoing.reshape(owners, resident_count, CAP, model_width)
    reduced_rows = jnp.einsum(
        "qtue,tve->qtuv",
        lax.all_to_all(outgoing, "adapt", split_axis=0, concat_axis=0, tiled=True),
        down,
        preferred_element_type=jnp.float32,
    ).astype(jnp.bfloat16)
    returned = lax.all_to_all(
        jnp.einsum("afok,fkx->afox", reduced_rows, up, preferred_element_type=jnp.float32).astype(
            jnp.bfloat16
        ),
        "adapt",
        split_axis=0,
        concat_axis=0,
        tiled=True,
    )
    update_rows = returned.reshape(owners * resident_count * CAP, model_width)[position]
    update_rows = update_rows.reshape(tok_rows, per_token, model_width)
    adapted_query_rows = (
        frozen_query[:, None, :].astype(jnp.float32)
        + ADAPTER_SCALE * update_rows.astype(jnp.float32)
    ).astype(jnp.bfloat16)
    return attend_all(adapted_query_rows, keys[0], values[0], cache_length[0])


def owner_kernel(folds, cap, rank, lid_ref, rows_ref, down_ref, up_ref, out_ref, part, squeezed):
    step = pl.program_id(0)
    total, width = part.shape
    block = folds * cap
    fold_of = (lax.broadcasted_iota(jnp.int32, (total, 1), 0) % block) // cap

    @pl.when(step < folds)
    def _():
        z = lax.dot_general(
            rows_ref[...],
            down_ref[...],
            (((1,), (1,)), ((), ())),
            preferred_element_type=jnp.float32,
        )
        lane = lax.broadcasted_iota(jnp.int32, (total, width), 1) // rank
        kept = jnp.where(lane == lid_ref[...], z, 0.0)
        part[...] = jnp.where(fold_of == step, kept, part[...])

    @pl.when(step == folds)
    def _():
        pairs = min(total, 16 * block)
        a = lax.broadcasted_iota(jnp.int32, (pairs, pairs), 0)
        b = lax.broadcasted_iota(jnp.int32, (pairs, pairs), 1)
        same = (a // block == b // block) & (a % cap == b % cap)
        mix = same.astype(jnp.float32)
        for start in range(0, total, pairs):
            squeezed[start : start + pairs, :] = lax.dot_general(
                mix,
                part[start : start + pairs, :],
                (((1,), (0,)), ((), ())),
                preferred_element_type=jnp.float32,
                precision=lax.Precision.HIGHEST,
            ).astype(jnp.bfloat16)

    @pl.when(step >= folds)
    def _():
        d = jnp.dot(squeezed[...], up_ref[...], preferred_element_type=jnp.float32)
        d = d.astype(jnp.bfloat16).astype(jnp.float32)
        old = out_ref[...].astype(jnp.float32)
        out_ref[...] = jnp.where(fold_of == step - folds, d, old).astype(jnp.bfloat16)


def owner_part(rows, lid, down, up, folds, cap):
    total, width = rows.shape
    resident, rank, model_width = down.shape
    ranks = resident * rank
    return pl.pallas_call(
        functools.partial(owner_kernel, folds, cap, rank),
        grid=(2 * folds,),
        in_specs=[
            pl.BlockSpec((total, 1), lambda i: (0, 0)),
            pl.BlockSpec((total, width), lambda i: (0, 0)),
            pl.BlockSpec((ranks, width), lambda i: (0, jnp.minimum(i, folds - 1))),
            pl.BlockSpec((ranks, width), lambda i: (0, jnp.maximum(i - folds, 0))),
        ],
        out_specs=pl.BlockSpec((total, width), lambda i: (0, 0)),
        out_shape=jax.ShapeDtypeStruct((total, width), jnp.bfloat16),
        scratch_shapes=[
            pltpu.VMEM((total, ranks), jnp.float32),
            pltpu.VMEM((total, ranks), jnp.bfloat16),
        ],
        compiler_params=pltpu.CompilerParams(vmem_limit_bytes=VMEM_LIMIT),
    )(lid, rows, down.reshape(ranks, model_width), up.reshape(ranks, model_width))


def attend_kernel(per_token, heads, cap, per_fold, cached_ref, pos_ref, ret_ref, frozen_ref,
                  key_ref, value_ref, out_ref, bias):
    g = pl.program_id(0)
    rows = pos_ref.shape[0]
    tokens = frozen_ref.shape[0]
    key_total = key_ref.shape[0]
    history = key_total - tokens

    @pl.when(g == 0)
    def _():
        j = lax.broadcasted_iota(jnp.int32, bias.shape, 1)
        t = (lax.broadcasted_iota(jnp.int32, bias.shape, 0) % rows) // per_token
        seen = (j >= history - cached_ref[0]) & (j <= history + t)
        bias[...] = jnp.where(seen, 0.0, -1e30)

    slots = ret_ref.shape[0]
    want = pos_ref[...] + (g // per_fold) * cap
    pick = (lax.broadcasted_iota(jnp.int32, (rows, slots), 1) == want)
    pick = pick.astype(jnp.float32).astype(jnp.bfloat16)
    update = jnp.dot(pick, ret_ref[...], preferred_element_type=jnp.float32)
    spread = (
        lax.broadcasted_iota(jnp.int32, (rows, tokens), 1)
        == lax.broadcasted_iota(jnp.int32, (rows, tokens), 0) // per_token
    )
    spread = spread.astype(jnp.float32).astype(jnp.bfloat16)
    base = jnp.dot(spread, frozen_ref[...], preferred_element_type=jnp.float32)
    query = (base + ADAPTER_SCALE * update).astype(jnp.bfloat16)
    scale = math.log2(math.e) / math.sqrt(HEAD)
    keys = key_ref[...]
    values = value_ref[...]
    for h in range(0, heads, 2):
        pair = jnp.concatenate(
            [query[:, h * HEAD : (h + 1) * HEAD], query[:, (h + 1) * HEAD : (h + 2) * HEAD]], axis=0
        )
        scores = lax.dot_general(
            pair, keys, (((1,), (1,)), ((), ())), preferred_element_type=jnp.float32
        )
        scores = scores + bias[...]
        peak = jnp.max(scores, axis=-1, keepdims=True)
        raised = jnp.exp2((scores - peak) * scale)
        whole = jnp.sum(raised, axis=-1, keepdims=True)
        mixed = jnp.dot(raised.astype(jnp.bfloat16), values, preferred_element_type=jnp.float32)
        mixed = (mixed / whole).astype(jnp.bfloat16)
        out_ref[:, h * HEAD : (h + 1) * HEAD] = mixed[:rows]
        out_ref[:, (h + 1) * HEAD : (h + 2) * HEAD] = mixed[rows:]


def attend_part(ret, pos, frozen_query, key_block, value_block, cached, per_token, cap):
    slots, width = ret.shape
    tokens, model_width = frozen_query.shape
    key_total, kv_width = key_block.shape
    kv_heads = kv_width // HEAD
    columns = model_width // kv_heads
    heads = columns // HEAD
    per_fold = width // columns
    rows = tokens * per_token
    return pl.pallas_call(
        functools.partial(attend_kernel, per_token, heads, cap, per_fold),
        grid=(kv_heads,),
        in_specs=[
            pl.BlockSpec(memory_space=pltpu.SMEM),
            pl.BlockSpec((rows, 1), lambda g: (0, 0)),
            pl.BlockSpec((slots, columns), lambda g: (0, g % per_fold)),
            pl.BlockSpec((tokens, columns), lambda g: (0, g)),
            pl.BlockSpec((key_total, HEAD), lambda g: (0, g)),
            pl.BlockSpec((key_total, HEAD), lambda g: (0, g)),
        ],
        out_specs=pl.BlockSpec((rows, columns), lambda g: (0, g)),
        out_shape=jax.ShapeDtypeStruct((rows, model_width), jnp.bfloat16),
        scratch_shapes=[pltpu.VMEM((2 * rows, key_total), jnp.float32)],
        compiler_params=pltpu.CompilerParams(vmem_limit_bytes=VMEM_LIMIT),
    )(cached, pos, ret, frozen_query, key_block, value_block)


def body(hidden, frozen_query, keys, values, cache_length, adapter_index, down, up):
    tokens, model_width = hidden.shape
    per_token = adapter_index.shape[1]
    rows = tokens * per_token
    resident = down.shape[0]
    owners = lax.axis_size("adapt")
    me = lax.axis_index("adapt")
    most = resident * CAP
    cap = most * 3 // 4 if most >= 16 else most
    folds = 16 // math.gcd(cap, 16)
    block = folds * cap
    width = model_width // folds
    slots = owners * block

    ids = adapter_index.reshape(rows)
    owner = ids // resident
    earlier = (
        lax.broadcasted_iota(jnp.int32, (rows, rows), 1)
        < lax.broadcasted_iota(jnp.int32, (rows, rows), 0)
    )
    slot = jnp.sum(((owner[:, None] == owner[None, :]) & earlier).astype(jnp.int32), axis=1)
    pos = owner * block + slot
    fits = slot < cap

    all_ids = lax.all_gather(adapter_index.reshape(1, rows), "adapt", axis=0, tiled=True)
    all_owner = all_ids // resident
    mine = all_owner == me
    rank_at = jnp.cumsum(mine.astype(jnp.int32), axis=1) - 1
    hit = mine[:, None, :] & (
        rank_at[:, None, :] == lax.broadcasted_iota(jnp.int32, (1, cap, 1), 1)
    )
    lid = jnp.sum(jnp.where(hit, all_ids[:, None, :] % resident + 1, 0), axis=2) - 1
    lid = jnp.broadcast_to(lid[:, None, :], (owners, folds, cap)).reshape(slots, 1)

    slot_index = lax.broadcasted_iota(jnp.int32, (slots, folds, tokens), 0)
    fold_index = lax.broadcasted_iota(jnp.int32, (slots, folds, tokens), 1)
    names = jnp.where(fits, pos, -1).reshape(tokens, per_token)
    pick = jnp.zeros((slots, folds, tokens), jnp.bool_)
    for k in range(per_token):
        pick = pick | (slot_index - fold_index * cap == names[:, k][None, None, :])
    pick = pick & ((slot_index % block) // cap == fold_index)
    pick = pick.astype(jnp.bfloat16).reshape(slots, folds * tokens)
    stacked = jnp.concatenate(
        [hidden[:, f * width : (f + 1) * width] for f in range(folds)], axis=0
    )
    outgoing = jnp.dot(pick, stacked, preferred_element_type=jnp.float32).astype(jnp.bfloat16)
    arrived = lax.all_to_all(
        outgoing.reshape(owners, block, width), "adapt", split_axis=0, concat_axis=0, tiled=True
    )

    def capped(arrived, lid, pos):
        delta = owner_part(arrived.reshape(slots, width), lid, down, up, folds, cap)
        returned = lax.all_to_all(
            delta.reshape(owners, block, width), "adapt", split_axis=0, concat_axis=0, tiled=True
        )
        context = attend_part(
            returned.reshape(slots, width),
            pos.reshape(rows, 1),
            frozen_query,
            keys[0],
            values[0],
            cache_length,
            per_token,
            cap,
        )
        return context.reshape(tokens, per_token, model_width)

    if cap == most:
        return capped(arrived, lid, pos)
    counts = jnp.sum(
        (
            all_owner[:, None, :]
            == lax.broadcasted_iota(jnp.int32, (1, owners, 1), 1)
        ).astype(jnp.int32),
        axis=2,
    )
    crowded = jnp.max(counts) > cap
    return lax.cond(
        crowded,
        lambda a, l, p: full_slots(
            hidden, frozen_query, keys, values, cache_length, adapter_index, down, up
        ),
        capped,
        arrived,
        lid,
        pos,
    )


def solution(mesh):
    rows2 = P(("groups", "adapt"), None)
    rows3 = P(("groups", "adapt"), None, None)
    in_specs = (rows2, rows2, rows3, rows3, P(("groups", "adapt")), rows2, rows3, rows3)
    return jax.shard_map(body, mesh=mesh, in_specs=in_specs, out_specs=rows3, check_vma=False)
```

time: 297 us -> 223 us (0.75)
  matrix products: 49.1 us -> 2.75 us
  Pallas kernels: 0 us -> 46 us
  local copies, waits for them, and re-layouts: 54.5 us -> 10.9 us
  blocking collectives: 98.9 us -> 79.1 us
  waiting for transfers between devices: 85.7 us -> 69.1 us
  starting transfers between devices: 5.46 us -> 11.7 us
    all_to_all x1 -> x0, blocking collectives: 98.9 us -> none  [body(): lax.all_to_all(outgoing, 'adapt', split_axis=0, concat_axis=0, tiled=True)]
    all_gather x0 -> x1, blocking collectives: none -> 79.1 us  [body(): lax.all_gather(adapter_index.reshape(1, rows), 'adapt', axis=0, tiled=True)]
    pallas_call x0 -> x2, Pallas kernels: none -> 46 us  [the longest x1 28.2 us: attend_part(): pl.pallas_call(functools.partial(attend_kernel, per_token, heads, cap, pe...]
    sub x1 -> x0, matrix products: 24.6 us -> none  [attend(): raised = jnp.where(visible, jnp.exp(scores - row_peak), 0.0)]
    dot_general x2 -> x1, matrix products: 24.5 us -> 2.75 us  [body(): jnp.dot(pick, stacked, preferred_element_type=jnp.float32)]
    all_to_all x1 -> x2, waiting for transfers between devices: 85.7 us -> 69.1 us  [the longest x1 69.1 us: capped(): lax.all_to_all(delta.reshape(owners, block, width), 'adapt', split_axis=0...]
    convert_element_type x3 -> x0, local copies, waits for them, and re-layouts: 11.1 us -> none  [the longest x1 8.52 us: body(): returned = lax.all_to_all(jnp.einsum('afok,fkx->afox', reduced_rows, adap...]
    reshape x3 -> x4, local copies, waits for them, and re-layouts: 17 us -> 6.17 us  [the longest x1 4.38 us: capped(): return context.reshape(tokens, per_token, model_width)]
  transfers between devices with their start and end apart: 1 -> 2, of which waited for: 1 -> 1; matrix products, arithmetic and copies ran while one was open for 2% -> 1% of each run, Pallas kernels for 0% -> 0%
where the time goes in v1:
time: 223 us
  blocking collectives  79.1 us (35%)
  waiting for transfers between devices  69.1 us (31%)
  Pallas kernels  46 us (21%)
  starting transfers between devices  11.7 us (5%)
  local copies, waits for them, and re-layouts  10.9 us (5%)
  matrix products  2.75 us (1%)
  other arithmetic  2.52 us (1%)
    all_gather x1, blocking collectives, body(): lax.all_gather(adapter_index.reshape(1, rows), 'adapt', axis=0, tiled=True)  79.1 us
    all_to_all x1, waiting for transfers between devices, capped(): lax.all_to_all(delta.reshape(owners, block, width), 'adapt', split_axis=0...  69.1 us
    pallas_call x1, Pallas kernels, attend_part(): pl.pallas_call(functools.partial(attend_kernel, per_token, heads, cap, pe...  28.2 us
    pallas_call x1, Pallas kernels, owner_part(): pl.pallas_call(functools.partial(owner_kernel, folds, cap, rank), grid=(2...  17.8 us
    all_to_all x1, starting transfers between devices, body(): lax.all_to_all(outgoing.reshape(owners, block, width), 'adapt', split_axi...  6.69 us
    all_to_all x1, starting transfers between devices, capped(): lax.all_to_all(delta.reshape(owners, block, width), 'adapt', split_axis=0...  4.99 us
  transfers between devices with their start and end apart: 2, of which 1 were waited for; matrix products, arithmetic and copies ran while one was open for 1% of the time, Pallas kernels for 0%

profile of v1, /device:TPU:15, one launch (start us, length us, event | category | flops | bytes accessed | tf_op | source)
XLA Modules:
  0.0 223.0 jit_solution(14403975704267827570)
XLA Ops:
  0.0 0.8 copy.124
  0.8 0.7 broadcast_compare_fusion.1
  1.5 0.1 reshape.202
  1.6 0.2 convert_reduce_fusion.2
  1.8 0.1 reduce_sum.52
  2.0 0.1 copy.131
  2.1 0.2 slice_reduce_fusion.1
  2.3 0.1 eq.114
  2.4 0.1 eq.119
  2.5 1.3 fusion.109
  3.7 0.1 iota.92
  3.8 0.1 iota.93
  3.9 0.1 iota.100
  4.0 2.8 %convolution_convert_fusion.1 = bf16[768,2048]{1,0:T(8,128)(2,1)} fusion(bf16[64,2048]{1,0:T(8,128)(2,1)S(1)} %get-tuple-element.300, bf16[64,2048]{1,0:T(8,128)(2,1)S(1)} %get-tuple-element.298, bf16[64,2048]{1,0:T(8,128)(2,1)S(1)} %get-tuple-element.299, bf16[64,2048]{1,0:T(8,128)(2,1)S(1)} %get-tuple-element.297, s32[256]{0:T(256)S(1)} %iota.100, ...), kind=kOutput, calls=%fused_computation.56 | convolution fusion | flops 814022656 | bytes 4205312 | tf_op jit(solution)/shard_map/dot_general | solution.py:271
  6.7 6.7 %all-to-all-start.3 = ((bf16[16,48,2048]{2,1,0:T(8,128)(2,1)}), bf16[16,48,2048]{2,1,0:T(8,128)(2,1)S(1)}, u32[]{:S(2)}, u32[]{:S(2)}) async-start(bf16[16,48,2048]{2,1,0:T(8,128)(2,1)} %bitcast.89), calls=%async_computation.3 | async-start | bytes 6291456 | tf_op jit(solution)/shard_map/all_to_all | solution.py:272
  13.4 0.1 reshape.222
  13.6 79.1 %all-gather = s32[16,1,128]{2,1,0:T(1,128)S(1)} all-gather(s32[1,1,128]{2,1,0:T(1,128)S(1)} %reshape.222), channel_id=1, replica_groups=mesh['groups'=2,'adapt'=16] {'adapt'}, dimensions={0}, use_global_device_ids=true | all-gather | bytes 8704 | tf_op jit(solution)/shard_map/all_gather | solution.py:250
  92.6 0.3 convert_reduce_fusion.1
  93.0 0.6 reduce_max.18
  94.3 0.3 reduce_window_sum.17
  94.6 0.0 all-to-all-done.3
  94.6 128.3 %conditional.1 = (bf16[64,2,8192]{2,1,0:T(2,128)(2,1)}) conditional(s32[]{:T(128)} %convert_element_type.53, (s32[128]{0:T(128)S(1)}, s32[128]{0:T(128)S(1)}, pred[128]{0:T(512)(128)(4,1)S(1)}, s32[128]{0:T(128)S(1)}, s32[128]{0:T(128)S(1)}, /*index=5*/s32[128]{0:T(128)S(1)}, pred[16,128]{1,0:T(8,128)(4,1)S(1)}, s32[16,1,128]{2,0,1:T(8,128)S(1)}, ...), branch_computations={%region_4.6_spmd, %region_6.11_spmd} | conditional | flops 4902325760 | bytes 233265952 | solution.py:303
  94.7 0.3 select_reduce_fusion
  95.0 0.1 copy.113
  95.1 0.9 reshape.229.lid_ref
  96.0 17.8 %branch_0_fun.2 = bf16[768,2048]{1,0:T(8,128)(2,1)} custom-call(s32[768,1]{1,0:T(8,128)} %reshape.229.lid_ref, bf16[768,2048]{1,0:T(8,128)(2,1)S(1)} %bitcast.81, bf16[256,8192]{1,0:T(8,128)(2,1)} %bitcast.79, bf16[256,8192]{1,0:T(8,128)(2,1)} %bitcast.80), custom_call_target="tpu_custom_call" | custom-call | tf_op jit(solution)/shard_map/cond/branch_0_fun/pallas_call | solution.py:133
  113.8 5.0 %all-to-all-start = ((bf16[16,48,2048]{2,1,0:T(8,128)(2,1)}), bf16[16,48,2048]{2,1,0:T(8,128)(2,1)S(1)}, u32[]{:S(2)}, u32[]{:S(2)}) async-start(bf16[16,48,2048]{2,1,0:T(8,128)(2,1)} %bitcast.82), calls=%async_computation | async-start | bytes 6291456 | tf_op jit(solution)/shard_map/cond/branch_0_fun/all_to_all | solution.py:278
  118.8 0.7 copy.115.pos_ref
  119.6 69.1 %all-to-all-done = bf16[16,48,2048]{2,1,0:T(8,128)(2,1)S(1)} async-done(((bf16[16,48,2048]{2,1,0:T(8,128)(2,1)}), bf16[16,48,2048]{2,1,0:T(8,128)(2,1)S(1)}, u32[]{:S(2)}, u32[]{:S(2)}) %all-to-all-start) | async-done | bytes 3145760 | tf_op jit(solution)/shard_map/cond/branch_0_fun/all_to_all | solution.py:278
  188.7 1.7 copy-done
  190.4 28.2 %branch_0_fun.3 = bf16[128,8192]{1,0:T(8,128)(2,1)} custom-call(s32[1]{0:T(128)} %get-tuple-element.113.cached_ref, s32[128,1]{1,0:T(8,128)} %copy.115.pos_ref, bf16[768,2048]{1,0:T(8,128)(2,1)} %bitcast.83, bf16[64,8192]{1,0:T(8,128)(2,1)} %get-tuple-element.129.frozen_ref, bf16[1088,1024]{1,0:T(8,128)(2,1)} %bitcast.84, bf16[1088,1024]{1,0:T(8,128)(2,1)} %bitcast.86), custom_call_target="tpu_custom_call" | custom-call | tf_op jit(solution)/shard_map/cond/branch_0_fun/pallas_call | solution.py:208
  218.6 4.4 %reshape.194 = bf16[64,2,8192]{2,1,0:T(2,128)(2,1)} reshape(bf16[128,8192]{1,0:T(8,128)(2,1)} %branch_0_fun.3) | data formatting | bytes 4194304 | tf_op jit(solution)/shard_map/cond/branch_0_fun/reshape | solution.py:291
  (23 shorter events, 0.1 us)
Async XLA Ops:
  6.7 87.9 %copy-start.5 = (s32[64,2]{0,1:T(2,128)S(1)}, s32[64,2]{0,1:T(2,128)}, u32[]{:S(2)}) copy-start(s32[64,2]{0,1:T(2,128)} %param.15) | copy-start | bytes 1540
  6.7 87.8 %all-to-all-start.3 = ((bf16[16,48,2048]{2,1,0:T(8,128)(2,1)}), bf16[16,48,2048]{2,1,0:T(8,128)(2,1)S(1)}, u32[]{:S(2)}, u32[]{:S(2)}) async-start(bf16[16,48,2048]{2,1,0:T(8,128)(2,1)} %bitcast.89), calls=%async_computation.3 | async-start | bytes 6291456 | tf_op jit(solution)/shard_map/all_to_all | solution.py:272
  113.8 74.9 %all-to-all-start = ((bf16[16,48,2048]{2,1,0:T(8,128)(2,1)}), bf16[16,48,2048]{2,1,0:T(8,128)(2,1)S(1)}, u32[]{:S(2)}, u32[]{:S(2)}) async-start(bf16[16,48,2048]{2,1,0:T(8,128)(2,1)} %bitcast.82), calls=%async_computation | async-start | bytes 6291456 | tf_op jit(solution)/shard_map/cond/branch_0_fun/all_to_all | solution.py:278
  188.7 1.7 copy-start

commit v2 on v1

--- a/solution.py
+++ b/solution.py
@@ -84,11 +84,22 @@
     return attend_all(adapted_query_rows, keys[0], values[0], cache_length[0])
 
 
-def owner_kernel(folds, cap, rank, lid_ref, rows_ref, down_ref, up_ref, out_ref, part, squeezed):
+def fold_column(total, folds, cap):
+    return (lax.broadcasted_iota(jnp.int32, (total, 1), 0) % (folds * cap)) // cap
+
+
+def raise_fold(fold, fold_of, squeezed_ref, up_ref, out_ref):
+    d = jnp.dot(squeezed_ref[...], up_ref[...], preferred_element_type=jnp.float32)
+    d = d.astype(jnp.bfloat16).astype(jnp.float32)
+    old = out_ref[...].astype(jnp.float32)
+    out_ref[...] = jnp.where(fold_of == fold, d, old).astype(jnp.bfloat16)
+
+
+def owner_kernel(folds, cap, rank, lid_ref, rows_ref, down_ref, up_ref, out_ref, squeezed, part):
     step = pl.program_id(0)
     total, width = part.shape
     block = folds * cap
-    fold_of = (lax.broadcasted_iota(jnp.int32, (total, 1), 0) % block) // cap
+    fold_of = fold_column(total, folds, cap)
 
     @pl.when(step < folds)
     def _():
@@ -120,16 +131,14 @@
 
     @pl.when(step >= folds)
     def _():
-        d = jnp.dot(squeezed[...], up_ref[...], preferred_element_type=jnp.float32)
-        d = d.astype(jnp.bfloat16).astype(jnp.float32)
-        old = out_ref[...].astype(jnp.float32)
-        out_ref[...] = jnp.where(fold_of == step - folds, d, old).astype(jnp.bfloat16)
-
-
-def owner_part(rows, lid, down, up, folds, cap):
+        raise_fold(step - folds, fold_of, squeezed, up_ref, out_ref)
+
+
+def owner_part(rows, lid, down, up, folds, cap, chunks):
     total, width = rows.shape
-    resident, rank, model_width = down.shape
-    ranks = resident * rank
+    ranks, model_width = up.shape
+    rank = ranks // (down.shape[0])
+    columns = width // chunks
     return pl.pallas_call(
         functools.partial(owner_kernel, folds, cap, rank),
         grid=(2 * folds,),
@@ -137,20 +146,51 @@
             pl.BlockSpec((total, 1), lambda i: (0, 0)),
             pl.BlockSpec((total, width), lambda i: (0, 0)),
             pl.BlockSpec((ranks, width), lambda i: (0, jnp.minimum(i, folds - 1))),
-            pl.BlockSpec((ranks, width), lambda i: (0, jnp.maximum(i - folds, 0))),
+            pl.BlockSpec((ranks, columns), lambda i: (0, jnp.maximum(i - folds, 0) * chunks)),
         ],
-        out_specs=pl.BlockSpec((total, width), lambda i: (0, 0)),
-        out_shape=jax.ShapeDtypeStruct((total, width), jnp.bfloat16),
-        scratch_shapes=[
-            pltpu.VMEM((total, ranks), jnp.float32),
-            pltpu.VMEM((total, ranks), jnp.bfloat16),
+        out_specs=[
+            pl.BlockSpec((total, columns), lambda i: (0, 0)),
+            pl.BlockSpec((total, ranks), lambda i: (0, 0)),
         ],
+        out_shape=[
+            jax.ShapeDtypeStruct((total, columns), jnp.bfloat16),
+            jax.ShapeDtypeStruct((total, ranks), jnp.bfloat16),
+        ],
+        scratch_shapes=[pltpu.VMEM((total, ranks), jnp.float32)],
+        cost_estimate=pl.CostEstimate(
+            flops=6 * total * ranks * model_width, bytes_accessed=40_000_000, transcendentals=0
+        ),
         compiler_params=pltpu.CompilerParams(vmem_limit_bytes=VMEM_LIMIT),
-    )(lid, rows, down.reshape(ranks, model_width), up.reshape(ranks, model_width))
-
-
-def attend_kernel(per_token, heads, cap, per_fold, cached_ref, pos_ref, ret_ref, frozen_ref,
-                  key_ref, value_ref, out_ref, bias):
+    )(lid, rows, down.reshape(ranks, model_width), up)
+
+
+def raise_kernel(folds, cap, squeezed_ref, up_ref, out_ref):
+    fold_of = fold_column(out_ref.shape[0], folds, cap)
+    raise_fold(pl.program_id(0), fold_of, squeezed_ref, up_ref, out_ref)
+
+
+def raise_part(squeezed, up, folds, cap, chunks, chunk):
+    total, ranks = squeezed.shape
+    columns = up.shape[1] // (folds * chunks)
+    return pl.pallas_call(
+        functools.partial(raise_kernel, folds, cap),
+        grid=(folds,),
+        in_specs=[
+            pl.BlockSpec((total, ranks), lambda i: (0, 0)),
+            pl.BlockSpec((ranks, columns), lambda i: (0, i * chunks + chunk)),
+        ],
+        out_specs=pl.BlockSpec((total, columns), lambda i: (0, 0)),
+        out_shape=jax.ShapeDtypeStruct((total, columns), jnp.bfloat16),
+        cost_estimate=pl.CostEstimate(
+            flops=2 * total * ranks * columns * folds, bytes_accessed=12_000_000, transcendentals=0
+        ),
+        compiler_params=pltpu.CompilerParams(vmem_limit_bytes=VMEM_LIMIT),
+    )(squeezed, up)
+
+
+def attend_kernel(per_token, heads, cap, cached_ref, pos_ref, ret_ref, frozen_ref, key_ref,
+                  value_ref, *rest):
+    out_ref, bias = rest[-2:]
     g = pl.program_id(0)
     rows = pos_ref.shape[0]
     tokens = frozen_ref.shape[0]
@@ -165,7 +205,7 @@
         bias[...] = jnp.where(seen, 0.0, -1e30)
 
     slots = ret_ref.shape[0]
-    want = pos_ref[...] + (g // per_fold) * cap
+    want = pos_ref[...] + g * cap
     pick = (lax.broadcasted_iota(jnp.int32, (rows, slots), 1) == want)
     pick = pick.astype(jnp.float32).astype(jnp.bfloat16)
     update = jnp.dot(pick, ret_ref[...], preferred_element_type=jnp.float32)
@@ -196,31 +236,44 @@
         out_ref[:, (h + 1) * HEAD : (h + 2) * HEAD] = mixed[rows:]
 
 
-def attend_part(ret, pos, frozen_query, key_block, value_block, cached, per_token, cap):
-    slots, width = ret.shape
+def attend_part(ret, pos, frozen_query, key_block, value_block, cached, per_token, cap, chunks,
+                chunk, before):
+    slots, columns = ret.shape
     tokens, model_width = frozen_query.shape
     key_total, kv_width = key_block.shape
-    kv_heads = kv_width // HEAD
-    columns = model_width // kv_heads
     heads = columns // HEAD
-    per_fold = width // columns
     rows = tokens * per_token
+    folds = model_width // (columns * chunks)
+    place = lambda g: (0, g * chunks + chunk)
+    operands = [cached, pos, ret, frozen_query, key_block, value_block]
+    in_specs = [
+        pl.BlockSpec(memory_space=pltpu.SMEM),
+        pl.BlockSpec((rows, 1), lambda g: (0, 0)),
+        pl.BlockSpec((slots, columns), lambda g: (0, 0)),
+        pl.BlockSpec((tokens, columns), place),
+        pl.BlockSpec((key_total, HEAD), place),
+        pl.BlockSpec((key_total, HEAD), place),
+    ]
+    aliases = {}
+    if before is not None:
+        aliases = {len(operands): 0}
+        operands.append(before)
+        in_specs.append(pl.BlockSpec(memory_space=pl.ANY))
     return pl.pallas_call(
-        functools.partial(attend_kernel, per_token, heads, cap, per_fold),
-        grid=(kv_heads,),
-        in_specs=[
-            pl.BlockSpec(memory_space=pltpu.SMEM),
-            pl.BlockSpec((rows, 1), lambda g: (0, 0)),
-            pl.BlockSpec((slots, columns), lambda g: (0, g % per_fold)),
-            pl.BlockSpec((tokens, columns), lambda g: (0, g)),
-            pl.BlockSpec((key_total, HEAD), lambda g: (0, g)),
-            pl.BlockSpec((key_total, HEAD), lambda g: (0, g)),
-        ],
-        out_specs=pl.BlockSpec((rows, columns), lambda g: (0, g)),
+        functools.partial(attend_kernel, per_token, heads, cap),
+        grid=(folds,),
+        in_specs=in_specs,
+        out_specs=pl.BlockSpec((rows, columns), place),
         out_shape=jax.ShapeDtypeStruct((rows, model_width), jnp.bfloat16),
         scratch_shapes=[pltpu.VMEM((2 * rows, key_total), jnp.float32)],
+        input_output_aliases=aliases,
+        cost_estimate=pl.CostEstimate(
+            flops=4 * rows * folds * columns * key_total,
+            bytes_accessed=40_000_000,
+            transcendentals=rows * heads * folds * key_total,
+        ),
         compiler_params=pltpu.CompilerParams(vmem_limit_bytes=VMEM_LIMIT),
-    )(cached, pos, ret, frozen_query, key_block, value_block)
+    )(*operands)
 
 
 def body(hidden, frozen_query, keys, values, cache_length, adapter_index, down, up):
@@ -236,6 +289,7 @@
     block = folds * cap
     width = model_width // folds
     slots = owners * block
+    chunks = width // (model_width // (keys.shape[2] // HEAD))
 
     ids = adapter_index.reshape(rows)
     owner = ids // resident
@@ -274,20 +328,38 @@
     )
 
     def capped(arrived, lid, pos):
-        delta = owner_part(arrived.reshape(slots, width), lid, down, up, folds, cap)
-        returned = lax.all_to_all(
-            delta.reshape(owners, block, width), "adapt", split_axis=0, concat_axis=0, tiled=True
+        flat_up = up.reshape(-1, model_width)
+        delta, squeezed = owner_part(
+            arrived.reshape(slots, width), lid, down, flat_up, folds, cap, chunks
         )
-        context = attend_part(
-            returned.reshape(slots, width),
-            pos.reshape(rows, 1),
-            frozen_query,
-            keys[0],
-            values[0],
-            cache_length,
-            per_token,
-            cap,
-        )
+        back = []
+        for chunk in range(chunks):
+            if chunk:
+                delta = raise_part(squeezed, flat_up, folds, cap, chunks, chunk)
+            back.append(
+                lax.all_to_all(
+                    delta.reshape(owners, block, width // chunks),
+                    "adapt",
+                    split_axis=0,
+                    concat_axis=0,
+                    tiled=True,
+                ).reshape(slots, width // chunks)
+            )
+        context = None
+        for chunk in range(chunks):
+            context = attend_part(
+                back[chunk],
+                pos.reshape(rows, 1),
+                frozen_query,
+                keys[0],
+                values[0],
+                cache_length,
+                per_token,
+                cap,
+                chunks,
+                chunk,
+                context,
+            )
         return context.reshape(tokens, per_token, model_width)
 
     if cap == most:

time: 223 us -> 216 us (0.969)
  waiting for transfers between devices: 69.1 us -> 50 us
  Pallas kernels: 46 us -> 54.3 us
  starting transfers between devices: 11.7 us -> 16.8 us
    all_to_all x1 -> x2, waiting for transfers between devices: 69.1 us -> 50 us  [capped(): lax.all_to_all(delta.reshape(owners, block, width // chunks), 'adapt', sp...]
    pallas_call x1 -> x3, Pallas kernels: 28.2 us -> 37.6 us  [the longest x2 31.5 us: attend_part(): pl.pallas_call(functools.partial(attend_kernel, per_token, heads, cap), g...]
    all_to_all x1 -> x2, starting transfers between devices: 4.99 us -> 9.96 us  [capped(): lax.all_to_all(delta.reshape(owners, block, width // chunks), 'adapt', sp...]
  transfers between devices with their start and end apart: 2 -> 3, of which waited for: 1 -> 2; matrix products, arithmetic and copies ran while one was open for 1% -> 1% of each run, Pallas kernels for 0% -> 10%
where the time goes in v2:
time: 216 us
  blocking collectives  79.1 us (37%)
  Pallas kernels  54.3 us (25%)
  waiting for transfers between devices  50 us (23%)
  starting transfers between devices  16.8 us (8%)
  local copies, waits for them, and re-layouts  9.29 us (4%)
  matrix products  2.75 us (1%)
  other arithmetic  2.51 us (1%)
    all_gather x1, blocking collectives, body(): lax.all_gather(adapter_index.reshape(1, rows), 'adapt', axis=0, tiled=True)  79.1 us
    all_to_all x2, waiting for transfers between devices, capped(): lax.all_to_all(delta.reshape(owners, block, width // chunks), 'adapt', sp...  50 us
    pallas_call x2, Pallas kernels, attend_part(): pl.pallas_call(functools.partial(attend_kernel, per_token, heads, cap), g...  31.5 us
    pallas_call x1, Pallas kernels, owner_part(): pl.pallas_call(functools.partial(owner_kernel, folds, cap, rank), grid=(2...  16.7 us
    all_to_all x2, starting transfers between devices, capped(): lax.all_to_all(delta.reshape(owners, block, width // chunks), 'adapt', sp...  9.96 us
    all_to_all x1, starting transfers between devices, body(): lax.all_to_all(outgoing.reshape(owners, block, width), 'adapt', split_axi...  6.82 us
    pallas_call x1, Pallas kernels, raise_part(): pl.pallas_call(functools.partial(raise_kernel, folds, cap), grid=(folds,)...  6.15 us
    reshape x1, local copies, waits for them, and re-layouts, capped(): return context.reshape(tokens, per_token, model_width)  4.38 us
  transfers between devices with their start and end apart: 3, of which 2 were waited for; matrix products, arithmetic and copies ran while one was open for 1% of the time, Pallas kernels for 10%

profile of v2, /device:TPU:15, one launch (start us, length us, event | category | flops | bytes accessed | tf_op | source)
XLA Modules:
  0.0 215.5 jit_solution(5106939700248712658)
XLA Ops:
  0.0 0.8 copy.126
  0.8 0.7 broadcast_compare_fusion.2
  1.5 0.1 reshape.211
  1.6 0.2 convert_reduce_fusion.2
  1.8 0.1 reduce_sum.51
  2.0 0.1 copy.133
  2.1 0.2 slice_reduce_fusion.1
  2.3 0.1 eq.106
  2.4 0.1 eq.111
  2.5 1.3 fusion.111
  3.8 0.1 iota.93
  3.9 0.1 iota.100
  4.0 2.8 %convolution_convert_fusion.1 = bf16[768,2048]{1,0:T(8,128)(2,1)} fusion(bf16[64,2048]{1,0:T(8,128)(2,1)S(1)} %get-tuple-element.163, bf16[64,2048]{1,0:T(8,128)(2,1)S(1)} %get-tuple-element.161, bf16[64,2048]{1,0:T(8,128)(2,1)S(1)} %get-tuple-element.162, bf16[64,2048]{1,0:T(8,128)(2,1)S(1)} %get-tuple-element.160, s32[256]{0:T(256)S(1)} %iota.100, ...), kind=kOutput, calls=%fused_computation.56 | convolution fusion | flops 814022656 | bytes 4205312 | tf_op jit(solution)/shard_map/dot_general | solution.py:325
  6.7 6.8 %all-to-all-start.4 = ((bf16[16,48,2048]{2,1,0:T(8,128)(2,1)}), bf16[16,48,2048]{2,1,0:T(8,128)(2,1)}, u32[]{:S(2)}, u32[]{:S(2)}) async-start(bf16[16,48,2048]{2,1,0:T(8,128)(2,1)} %bitcast.88), calls=%async_computation.4 | async-start | bytes 6291456 | tf_op jit(solution)/shard_map/all_to_all | solution.py:326
  13.6 0.1 reshape.232
  13.7 79.1 %all-gather = s32[16,1,128]{2,1,0:T(1,128)S(1)} all-gather(s32[1,1,128]{2,1,0:T(1,128)S(1)} %reshape.232), channel_id=1, replica_groups=mesh['groups'=2,'adapt'=16] {'adapt'}, dimensions={0}, use_global_device_ids=true | all-gather | bytes 8704 | tf_op jit(solution)/shard_map/all_gather | solution.py:304
  92.8 0.3 convert_reduce_fusion.1
  93.2 0.6 reduce_max.18
  94.5 0.3 reduce_window_sum.11
  94.8 120.7 %conditional.1 = (bf16[64,2,8192]{2,1,0:T(2,128)(2,1)}) conditional(s32[]{:T(128)} %convert_element_type.55, (s32[128]{0:T(128)S(1)}, bf16[16,48,2048]{2,1,0:T(8,128)(2,1)}, bf16[8,32,8192]{2,1,0:T(8,128)(2,1)}, bf16[8,32,8192]{2,1,0:T(8,128)(2,1)}, pred[16,128]{1,0:T(8,128)(4,1)S(1)}, /*index=5*/bf16[1,1088,1024]{2,1,0:T(8,128)(2,1)S(1)}, ...), branch_computations={%region_5.6_spmd, %region_6.11_spmd} | conditional | flops 15837802496 | bytes 220158688 | solution.py:375
  94.9 0.3 select_reduce_fusion
  95.3 0.9 reshape.239.lid_ref
  96.2 16.7 %branch_0_fun.4 = (bf16[768,1024]{1,0:T(8,128)(2,1)}, bf16[768,256]{1,0:T(8,128)(2,1)}) custom-call(s32[768,1]{1,0:T(8,128)} %reshape.239.lid_ref, bf16[768,2048]{1,0:T(8,128)(2,1)} %bitcast.1.rows_ref, bf16[256,8192]{1,0:T(8,128)(2,1)} %bitcast.87, bf16[256,8192]{1,0:T(8,128)(2,1)} %bitcast.83), custom_call_target="tpu_custom_call" | custom-call | flops 9663676416 | bytes 40000000 | tf_op jit(solution)/shard_map/cond/branch_0_fun/pallas_call | solution.py:142
  112.9 5.0 %all-to-all-start.1 = ((bf16[16,48,1024]{2,1,0:T(8,128)(2,1)}), bf16[16,48,1024]{2,1,0:T(8,128)(2,1)}, u32[]{:S(2)}, u32[]{:S(2)}) async-start(bf16[16,48,1024]{2,1,0:T(8,128)(2,1)} %bitcast.92), calls=%async_computation.1 | async-start | bytes 3145728 | tf_op jit(solution)/shard_map/cond/branch_0_fun/all_to_all | solution.py:340
  117.8 6.2 %branch_0_fun.5 = bf16[768,1024]{1,0:T(8,128)(2,1)} custom-call(bf16[768,256]{1,0:T(8,128)(2,1)} %get-tuple-element.48.squeezed_ref, bf16[256,8192]{1,0:T(8,128)(2,1)} %bitcast.84), custom_call_target="tpu_custom_call" | custom-call | flops 1610612736 | bytes 12000000 | tf_op jit(solution)/shard_map/cond/branch_0_fun/pallas_call | solution.py:175
  124.0 30.2 %all-to-all-done.1 = bf16[16,48,1024]{2,1,0:T(8,128)(2,1)} async-done(((bf16[16,48,1024]{2,1,0:T(8,128)(2,1)}), bf16[16,48,1024]{2,1,0:T(8,128)(2,1)}, u32[]{:S(2)}, u32[]{:S(2)}) %all-to-all-start.1) | async-done | bytes 1572896 | tf_op jit(solution)/shard_map/cond/branch_0_fun/all_to_all | solution.py:340
  154.1 5.0 %all-to-all-start = ((bf16[16,48,1024]{2,1,0:T(8,128)(2,1)}), bf16[16,48,1024]{2,1,0:T(8,128)(2,1)}, u32[]{:S(2)}, u32[]{:S(2)}) async-start(bf16[16,48,1024]{2,1,0:T(8,128)(2,1)} %bitcast.85), calls=%async_computation | async-start | bytes 3145728 | tf_op jit(solution)/shard_map/cond/branch_0_fun/all_to_all | solution.py:340
  159.1 0.7 copy.117.pos_ref
  159.9 15.7 %branch_0_fun.6.rest_0_ = bf16[128,8192]{1,0:T(8,128)(2,1)} custom-call(s32[1]{0:T(128)} %get-tuple-element.42.cached_ref, s32[128,1]{1,0:T(8,128)} %copy.117.pos_ref, bf16[768,1024]{1,0:T(8,128)(2,1)} %bitcast.9.ret_ref, bf16[64,8192]{1,0:T(8,128)(2,1)S(1)} %get-tuple-element.49.frozen_ref, bf16[1088,1024]{1,0:T(8,128)(2,1)S(1)} %bitcast.77, ...), custom_call_target="tpu_custom_call" | custom-call | flops 2281701376 | bytes 40000000 | tf_op jit(solution)/shard_map/cond/branch_0_fun/pallas_call | solution.py:262
  175.6 19.8 %all-to-all-done = bf16[16,48,1024]{2,1,0:T(8,128)(2,1)} async-done(((bf16[16,48,1024]{2,1,0:T(8,128)(2,1)}), bf16[16,48,1024]{2,1,0:T(8,128)(2,1)}, u32[]{:S(2)}, u32[]{:S(2)}) %all-to-all-start) | async-done | bytes 1572896 | tf_op jit(solution)/shard_map/cond/branch_0_fun/all_to_all | solution.py:340
  195.4 15.7 %branch_0_fun.7 = bf16[128,8192]{1,0:T(8,128)(2,1)} custom-call(s32[1]{0:T(128)} %get-tuple-element.42.cached_ref, s32[128,1]{1,0:T(8,128)} %copy.117.pos_ref, bf16[768,1024]{1,0:T(8,128)(2,1)} %bitcast.5.ret_ref, bf16[64,8192]{1,0:T(8,128)(2,1)S(1)} %get-tuple-element.49.frozen_ref, ...), custom_call_target="tpu_custom_call", output_to_operand_aliasing={{}: (6, {})} | custom-call | flops 2281701376 | bytes 40000000 | tf_op jit(solution)/shard_map/cond/branch_0_fun/pallas_call | solution.py:262
  211.1 4.4 %reshape.202 = bf16[64,2,8192]{2,1,0:T(2,128)(2,1)} reshape(bf16[128,8192]{1,0:T(8,128)(2,1)} %branch_0_fun.7) | data formatting | bytes 4194304 | tf_op jit(solution)/shard_map/cond/branch_0_fun/reshape | solution.py:363
  (28 shorter events, 0.3 us)
Async XLA Ops:
  6.7 88.1 %copy-start = (bf16[1,1088,1024]{2,1,0:T(8,128)(2,1)S(1)}, bf16[1,1088,1024]{2,1,0:T(8,128)(2,1)}, u32[]{:S(2)}) copy-start(bf16[1,1088,1024]{2,1,0:T(8,128)(2,1)} %param.12) | copy-start | bytes 6684676
  6.7 88.1 %copy-start.2 = (bf16[64,8192]{1,0:T(8,128)(2,1)S(1)}, bf16[64,8192]{1,0:T(8,128)(2,1)}, u32[]{:S(2)}) copy-start(bf16[64,8192]{1,0:T(8,128)(2,1)} %param.11) | copy-start | bytes 3145732
  6.7 88.1 %copy-start.4 = (s32[64,2]{0,1:T(2,128)S(1)}, s32[64,2]{0,1:T(2,128)}, u32[]{:S(2)}) copy-start(s32[64,2]{0,1:T(2,128)} %param.15) | copy-start | bytes 1540
  6.7 88.0 %all-to-all-start.4 = ((bf16[16,48,2048]{2,1,0:T(8,128)(2,1)}), bf16[16,48,2048]{2,1,0:T(8,128)(2,1)}, u32[]{:S(2)}, u32[]{:S(2)}) async-start(bf16[16,48,2048]{2,1,0:T(8,128)(2,1)} %bitcast.88), calls=%async_computation.4 | async-start | bytes 6291456 | tf_op jit(solution)/shard_map/all_to_all | solution.py:326
  112.9 41.3 %all-to-all-start.1 = ((bf16[16,48,1024]{2,1,0:T(8,128)(2,1)}), bf16[16,48,1024]{2,1,0:T(8,128)(2,1)}, u32[]{:S(2)}, u32[]{:S(2)}) async-start(bf16[16,48,1024]{2,1,0:T(8,128)(2,1)} %bitcast.92), calls=%async_computation.1 | async-start | bytes 3145728 | tf_op jit(solution)/shard_map/cond/branch_0_fun/all_to_all | solution.py:340
  154.1 41.3 %all-to-all-start = ((bf16[16,48,1024]{2,1,0:T(8,128)(2,1)}), bf16[16,48,1024]{2,1,0:T(8,128)(2,1)}, u32[]{:S(2)}, u32[]{:S(2)}) async-start(bf16[16,48,1024]{2,1,0:T(8,128)(2,1)} %bitcast.85), calls=%async_computation | async-start | bytes 3145728 | tf_op jit(solution)/shard_map/cond/branch_0_fun/all_to_all | solution.py:340

commit v3 on v2

--- a/solution.py
+++ b/solution.py
@@ -12,6 +12,7 @@
 CAP = 2
 ADAPTER_SCALE = 0.5
 VMEM_LIMIT = 56 * 1024 * 1024
+TILE = 512
 
 
 def attend_all(adapted_query_rows, key_block, value_block, cached):
@@ -88,14 +89,15 @@
     return (lax.broadcasted_iota(jnp.int32, (total, 1), 0) % (folds * cap)) // cap
 
 
-def raise_fold(fold, fold_of, squeezed_ref, up_ref, out_ref):
-    d = jnp.dot(squeezed_ref[...], up_ref[...], preferred_element_type=jnp.float32)
-    d = d.astype(jnp.bfloat16).astype(jnp.float32)
-    old = out_ref[...].astype(jnp.float32)
-    out_ref[...] = jnp.where(fold_of == fold, d, old).astype(jnp.bfloat16)
-
-
-def owner_kernel(folds, cap, rank, lid_ref, rows_ref, down_ref, up_ref, out_ref, squeezed, part):
+def raise_tile(blocked_ref, up_refs, out_ref):
+    ups = jnp.concatenate([u[...] for u in up_refs], axis=0)
+    d = jnp.dot(blocked_ref[...], ups, preferred_element_type=jnp.float32)
+    out_ref[...] = d.astype(jnp.bfloat16)
+
+
+def owner_kernel(folds, cap, rank, lid_ref, rows_ref, down_ref, *rest):
+    up_refs = rest[:folds]
+    out_ref, blocked, part = rest[folds:]
     step = pl.program_id(0)
     total, width = part.shape
     block = folds * cap
@@ -115,23 +117,28 @@
 
     @pl.when(step == folds)
     def _():
-        pairs = min(total, 16 * block)
-        a = lax.broadcasted_iota(jnp.int32, (pairs, pairs), 0)
-        b = lax.broadcasted_iota(jnp.int32, (pairs, pairs), 1)
-        same = (a // block == b // block) & (a % cap == b % cap)
+        pairs = min(total, 4 * block)
+        a = lax.broadcasted_iota(jnp.int32, (pairs, 1), 0)
+        b = lax.broadcasted_iota(jnp.int32, (1, pairs), 1)
+        same = (a // block) * cap + a % cap == (b // block) * cap + b % cap
         mix = same.astype(jnp.float32)
         for start in range(0, total, pairs):
-            squeezed[start : start + pairs, :] = lax.dot_general(
+            sums = lax.dot_general(
                 mix,
                 part[start : start + pairs, :],
                 (((1,), (0,)), ((), ())),
                 preferred_element_type=jnp.float32,
                 precision=lax.Precision.HIGHEST,
-            ).astype(jnp.bfloat16)
+            )
+            folded = fold_of[start : start + pairs]
+            for f in range(folds):
+                blocked[start : start + pairs, f * width : (f + 1) * width] = jnp.where(
+                    folded == f, sums, 0.0
+                ).astype(jnp.bfloat16)
 
     @pl.when(step >= folds)
     def _():
-        raise_fold(step - folds, fold_of, squeezed, up_ref, out_ref)
+        raise_tile(blocked, up_refs, out_ref)
 
 
 def owner_part(rows, lid, down, up, folds, cap, chunks):
@@ -139,53 +146,64 @@
     ranks, model_width = up.shape
     rank = ranks // (down.shape[0])
     columns = width // chunks
+    tile = min(columns, TILE)
+    tiles = columns // tile
     return pl.pallas_call(
         functools.partial(owner_kernel, folds, cap, rank),
-        grid=(2 * folds,),
+        grid=(folds + tiles,),
         in_specs=[
             pl.BlockSpec((total, 1), lambda i: (0, 0)),
             pl.BlockSpec((total, width), lambda i: (0, 0)),
             pl.BlockSpec((ranks, width), lambda i: (0, jnp.minimum(i, folds - 1))),
-            pl.BlockSpec((ranks, columns), lambda i: (0, jnp.maximum(i - folds, 0) * chunks)),
+        ]
+        + [
+            pl.BlockSpec(
+                (ranks, tile),
+                lambda i, f=f: (0, f * chunks * tiles + jnp.maximum(i - folds, 0)),
+            )
+            for f in range(folds)
         ],
         out_specs=[
-            pl.BlockSpec((total, columns), lambda i: (0, 0)),
-            pl.BlockSpec((total, ranks), lambda i: (0, 0)),
+            pl.BlockSpec((total, tile), lambda i: (0, jnp.maximum(i - folds, 0))),
+            pl.BlockSpec((total, folds * ranks), lambda i: (0, 0)),
         ],
         out_shape=[
             jax.ShapeDtypeStruct((total, columns), jnp.bfloat16),
-            jax.ShapeDtypeStruct((total, ranks), jnp.bfloat16),
+            jax.ShapeDtypeStruct((total, folds * ranks), jnp.bfloat16),
         ],
         scratch_shapes=[pltpu.VMEM((total, ranks), jnp.float32)],
         cost_estimate=pl.CostEstimate(
             flops=6 * total * ranks * model_width, bytes_accessed=40_000_000, transcendentals=0
         ),
         compiler_params=pltpu.CompilerParams(vmem_limit_bytes=VMEM_LIMIT),
-    )(lid, rows, down.reshape(ranks, model_width), up)
-
-
-def raise_kernel(folds, cap, squeezed_ref, up_ref, out_ref):
-    fold_of = fold_column(out_ref.shape[0], folds, cap)
-    raise_fold(pl.program_id(0), fold_of, squeezed_ref, up_ref, out_ref)
-
-
-def raise_part(squeezed, up, folds, cap, chunks, chunk):
-    total, ranks = squeezed.shape
-    columns = up.shape[1] // (folds * chunks)
+    )(lid, rows, down.reshape(ranks, model_width), *([up] * folds))
+
+
+def raise_kernel(folds, blocked_ref, *rest):
+    raise_tile(blocked_ref, rest[:folds], rest[folds])
+
+
+def raise_part(blocked, up, folds, chunks, chunk):
+    total = blocked.shape[0]
+    ranks, model_width = up.shape
+    columns = model_width // (folds * chunks)
+    tile = min(columns, TILE)
+    tiles = columns // tile
     return pl.pallas_call(
-        functools.partial(raise_kernel, folds, cap),
-        grid=(folds,),
-        in_specs=[
-            pl.BlockSpec((total, ranks), lambda i: (0, 0)),
-            pl.BlockSpec((ranks, columns), lambda i: (0, i * chunks + chunk)),
+        functools.partial(raise_kernel, folds),
+        grid=(tiles,),
+        in_specs=[pl.BlockSpec((total, folds * ranks), lambda i: (0, 0))]
+        + [
+            pl.BlockSpec((ranks, tile), lambda i, f=f: (0, (f * chunks + chunk) * tiles + i))
+            for f in range(folds)
         ],
-        out_specs=pl.BlockSpec((total, columns), lambda i: (0, 0)),
+        out_specs=pl.BlockSpec((total, tile), lambda i: (0, i)),
         out_shape=jax.ShapeDtypeStruct((total, columns), jnp.bfloat16),
         cost_estimate=pl.CostEstimate(
             flops=2 * total * ranks * columns * folds, bytes_accessed=12_000_000, transcendentals=0
         ),
         compiler_params=pltpu.CompilerParams(vmem_limit_bytes=VMEM_LIMIT),
-    )(squeezed, up)
+    )(blocked, *([up] * folds))
 
 
 def attend_kernel(per_token, heads, cap, cached_ref, pos_ref, ret_ref, frozen_ref, key_ref,
@@ -218,7 +236,7 @@
     query = (base + ADAPTER_SCALE * update).astype(jnp.bfloat16)
     scale = math.log2(math.e) / math.sqrt(HEAD)
     keys = key_ref[...]
-    values = value_ref[...]
+    values = jnp.concatenate([value_ref[...], jnp.ones_like(value_ref)], axis=1)
     for h in range(0, heads, 2):
         pair = jnp.concatenate(
             [query[:, h * HEAD : (h + 1) * HEAD], query[:, (h + 1) * HEAD : (h + 2) * HEAD]], axis=0
@@ -229,9 +247,8 @@
         scores = scores + bias[...]
         peak = jnp.max(scores, axis=-1, keepdims=True)
         raised = jnp.exp2((scores - peak) * scale)
-        whole = jnp.sum(raised, axis=-1, keepdims=True)
         mixed = jnp.dot(raised.astype(jnp.bfloat16), values, preferred_element_type=jnp.float32)
-        mixed = (mixed / whole).astype(jnp.bfloat16)
+        mixed = (mixed[:, :HEAD] / mixed[:, HEAD:]).astype(jnp.bfloat16)
         out_ref[:, h * HEAD : (h + 1) * HEAD] = mixed[:rows]
         out_ref[:, (h + 1) * HEAD : (h + 2) * HEAD] = mixed[rows:]
 
@@ -335,7 +352,7 @@
         back = []
         for chunk in range(chunks):
             if chunk:
-                delta = raise_part(squeezed, flat_up, folds, cap, chunks, chunk)
+                delta = raise_part(squeezed, flat_up, folds, chunks, chunk)
             back.append(
                 lax.all_to_all(
                     delta.reshape(owners, block, width // chunks),

time: 216 us -> 212 us (0.981)
  Pallas kernels: 54.3 us -> 46.7 us
  waiting for transfers between devices: 50 us -> 53.3 us
    pallas_call x2, Pallas kernels: 31.5 us -> 27.3 us  [attend_part(): pl.pallas_call(functools.partial(attend_kernel, per_token, heads, cap), g...]
    pallas_call x2, Pallas kernels: 22.8 us -> 19.4 us  [the longest x1 14.5 us: owner_part(): pl.pallas_call(functools.partial(owner_kernel, folds, cap, rank), grid=(f...]
    all_to_all x2, waiting for transfers between devices: 50 us -> 53.3 us  [capped(): lax.all_to_all(delta.reshape(owners, block, width // chunks), 'adapt', sp...]
  transfers between devices with their start and end apart: 3 -> 3, of which waited for: 2 -> 2; matrix products, arithmetic and copies ran while one was open for 1% -> 1% of each run, Pallas kernels for 10% -> 9%
where the time goes in v3:
time: 212 us; the launch traced here: 211 us
  blocking collectives  79.1 us (37%)
  waiting for transfers between devices  53.3 us (25%)
  Pallas kernels  46.7 us (22%)
  starting transfers between devices  16.8 us (8%)
  local copies, waits for them, and re-layouts  9.28 us (4%)
  matrix products  2.75 us (1%)
  other arithmetic  2.51 us (1%)
    all_gather x1, blocking collectives, body(): lax.all_gather(adapter_index.reshape(1, rows), 'adapt', axis=0, tiled=True)  79.1 us
    all_to_all x2, waiting for transfers between devices, capped(): lax.all_to_all(delta.reshape(owners, block, width // chunks), 'adapt', sp...  53.3 us
    pallas_call x2, Pallas kernels, attend_part(): pl.pallas_call(functools.partial(attend_kernel, per_token, heads, cap), g...  27.3 us
    pallas_call x1, Pallas kernels, owner_part(): pl.pallas_call(functools.partial(owner_kernel, folds, cap, rank), grid=(f...  14.5 us
    all_to_all x2, starting transfers between devices, capped(): lax.all_to_all(delta.reshape(owners, block, width // chunks), 'adapt', sp...  9.99 us
    all_to_all x1, starting transfers between devices, body(): lax.all_to_all(outgoing.reshape(owners, block, width), 'adapt', split_axi...  6.82 us
    pallas_call x1, Pallas kernels, raise_part(): pl.pallas_call(functools.partial(raise_kernel, folds), grid=(tiles,), in_...  4.88 us
    reshape x1, local copies, waits for them, and re-layouts, capped(): return context.reshape(tokens, per_token, model_width)  4.38 us
  transfers between devices with their start and end apart: 3, of which 2 were waited for; matrix products, arithmetic and copies ran while one was open for 1% of the time, Pallas kernels for 9%

profile of v3, /device:TPU:15, one launch (start us, length us, event | category | flops | bytes accessed | tf_op | source)
XLA Modules:
  0.0 211.3 jit_solution(524150418432504952)
XLA Ops:
  0.0 0.8 copy.126
  0.8 0.7 broadcast_compare_fusion.2
  1.5 0.1 reshape.211
  1.6 0.2 convert_reduce_fusion.2
  1.8 0.1 reduce_sum.51
  2.0 0.1 copy.133
  2.1 0.2 slice_reduce_fusion.1
  2.3 0.1 eq.106
  2.4 0.1 eq.111
  2.5 1.3 fusion.111
  3.8 0.1 iota.93
  3.9 0.1 iota.100
  4.0 2.8 %convolution_convert_fusion.1 = bf16[768,2048]{1,0:T(8,128)(2,1)} fusion(bf16[64,2048]{1,0:T(8,128)(2,1)S(1)} %get-tuple-element.163, bf16[64,2048]{1,0:T(8,128)(2,1)S(1)} %get-tuple-element.161, bf16[64,2048]{1,0:T(8,128)(2,1)S(1)} %get-tuple-element.162, bf16[64,2048]{1,0:T(8,128)(2,1)S(1)} %get-tuple-element.160, s32[256]{0:T(256)S(1)} %iota.100, ...), kind=kOutput, calls=%fused_computation.56 | convolution fusion | flops 814022656 | bytes 4205312 | tf_op jit(solution)/shard_map/dot_general | solution.py:342
  6.7 6.8 %all-to-all-start.4 = ((bf16[16,48,2048]{2,1,0:T(8,128)(2,1)}), bf16[16,48,2048]{2,1,0:T(8,128)(2,1)}, u32[]{:S(2)}, u32[]{:S(2)}) async-start(bf16[16,48,2048]{2,1,0:T(8,128)(2,1)} %bitcast.94), calls=%async_computation.4 | async-start | bytes 6291456 | tf_op jit(solution)/shard_map/all_to_all | solution.py:343
  13.6 0.1 reshape.232
  13.7 79.1 %all-gather = s32[16,1,128]{2,1,0:T(1,128)S(1)} all-gather(s32[1,1,128]{2,1,0:T(1,128)S(1)} %reshape.232), channel_id=1, replica_groups=mesh['groups'=2,'adapt'=16] {'adapt'}, dimensions={0}, use_global_device_ids=true | all-gather | bytes 8704 | tf_op jit(solution)/shard_map/all_gather | solution.py:321
  92.8 0.3 convert_reduce_fusion.1
  93.2 0.6 reduce_max.18
  94.5 0.3 reduce_window_sum.11
  94.8 116.4 %conditional.1 = (bf16[64,2,8192]{2,1,0:T(2,128)(2,1)}) conditional(s32[]{:T(128)} %convert_element_type.55, (s32[128]{0:T(128)S(1)}, bf16[16,48,2048]{2,1,0:T(8,128)(2,1)}, bf16[8,32,8192]{2,1,0:T(8,128)(2,1)}, bf16[8,32,8192]{2,1,0:T(8,128)(2,1)}, pred[16,128]{1,0:T(8,128)(4,1)S(1)}, /*index=5*/bf16[1,1088,1024]{2,1,0:T(8,128)(2,1)S(1)}, ...), branch_computations={%region_5.6_spmd, %region_6.11_spmd} | conditional | flops 15837802496 | bytes 220158688 | solution.py:392
  94.9 0.3 select_reduce_fusion
  95.3 0.9 reshape.239.lid_ref
  96.2 14.5 %branch_0_fun.4 = (bf16[768,1024]{1,0:T(8,128)(2,1)}, bf16[768,1024]{1,0:T(8,128)(2,1)}) custom-call(s32[768,1]{1,0:T(8,128)} %reshape.239.lid_ref, bf16[768,2048]{1,0:T(8,128)(2,1)} %bitcast.1.rows_ref, bf16[256,8192]{1,0:T(8,128)(2,1)} %bitcast.93, bf16[256,8192]{1,0:T(8,128)(2,1)} %bitcast.77, bf16[256,8192]{1,0:T(8,128)(2,1)} %bitcast.78, ...), custom_call_target="tpu_custom_call" | custom-call | flops 9663676416 | bytes 40000000 | tf_op jit(solution)/shard_map/cond/branch_0_fun/pallas_call | solution.py:151
  110.7 5.0 %all-to-all-start.1 = ((bf16[16,48,1024]{2,1,0:T(8,128)(2,1)}), bf16[16,48,1024]{2,1,0:T(8,128)(2,1)}, u32[]{:S(2)}, u32[]{:S(2)}) async-start(bf16[16,48,1024]{2,1,0:T(8,128)(2,1)} %bitcast.98), calls=%async_computation.1 | async-start | bytes 3145728 | tf_op jit(solution)/shard_map/cond/branch_0_fun/all_to_all | solution.py:357
  115.6 4.9 %branch_0_fun.5 = bf16[768,1024]{1,0:T(8,128)(2,1)} custom-call(bf16[768,1024]{1,0:T(8,128)(2,1)} %get-tuple-element.48.blocked_ref, bf16[256,8192]{1,0:T(8,128)(2,1)} %bitcast.81, bf16[256,8192]{1,0:T(8,128)(2,1)} %bitcast.82, bf16[256,8192]{1,0:T(8,128)(2,1)} %bitcast.83, bf16[256,8192]{1,0:T(8,128)(2,1)} %bitcast.84), custom_call_target="tpu_custom_call" | custom-call | flops 1610612736 | bytes 12000000 | tf_op jit(solution)/shard_map/cond/branch_0_fun/pallas_call | solution.py:192
  120.5 31.4 %all-to-all-done.1 = bf16[16,48,1024]{2,1,0:T(8,128)(2,1)} async-done(((bf16[16,48,1024]{2,1,0:T(8,128)(2,1)}), bf16[16,48,1024]{2,1,0:T(8,128)(2,1)}, u32[]{:S(2)}, u32[]{:S(2)}) %all-to-all-start.1) | async-done | bytes 1572896 | tf_op jit(solution)/shard_map/cond/branch_0_fun/all_to_all | solution.py:357
  151.9 5.0 %all-to-all-start = ((bf16[16,48,1024]{2,1,0:T(8,128)(2,1)}), bf16[16,48,1024]{2,1,0:T(8,128)(2,1)}, u32[]{:S(2)}, u32[]{:S(2)}) async-start(bf16[16,48,1024]{2,1,0:T(8,128)(2,1)} %bitcast.91), calls=%async_computation | async-start | bytes 3145728 | tf_op jit(solution)/shard_map/cond/branch_0_fun/all_to_all | solution.py:357
  157.0 0.7 copy.117.pos_ref
  157.7 13.7 %branch_0_fun.6.rest_0_ = bf16[128,8192]{1,0:T(8,128)(2,1)} custom-call(s32[1]{0:T(128)} %get-tuple-element.42.cached_ref, s32[128,1]{1,0:T(8,128)} %copy.117.pos_ref, bf16[768,1024]{1,0:T(8,128)(2,1)} %bitcast.9.ret_ref, bf16[64,8192]{1,0:T(8,128)(2,1)S(1)} %get-tuple-element.49.frozen_ref, bf16[1088,1024]{1,0:T(8,128)(2,1)S(1)} %bitcast.85, ...), custom_call_target="tpu_custom_call" | custom-call | flops 2281701376 | bytes 40000000 | tf_op jit(solution)/shard_map/cond/branch_0_fun/pallas_call | solution.py:279
  171.4 21.9 %all-to-all-done = bf16[16,48,1024]{2,1,0:T(8,128)(2,1)} async-done(((bf16[16,48,1024]{2,1,0:T(8,128)(2,1)}), bf16[16,48,1024]{2,1,0:T(8,128)(2,1)}, u32[]{:S(2)}, u32[]{:S(2)}) %all-to-all-start) | async-done | bytes 1572896 | tf_op jit(solution)/shard_map/cond/branch_0_fun/all_to_all | solution.py:357
  193.2 13.7 %branch_0_fun.7 = bf16[128,8192]{1,0:T(8,128)(2,1)} custom-call(s32[1]{0:T(128)} %get-tuple-element.42.cached_ref, s32[128,1]{1,0:T(8,128)} %copy.117.pos_ref, bf16[768,1024]{1,0:T(8,128)(2,1)} %bitcast.5.ret_ref, bf16[64,8192]{1,0:T(8,128)(2,1)S(1)} %get-tuple-element.49.frozen_ref, ...), custom_call_target="tpu_custom_call", output_to_operand_aliasing={{}: (6, {})} | custom-call | flops 2281701376 | bytes 40000000 | tf_op jit(solution)/shard_map/cond/branch_0_fun/pallas_call | solution.py:279
  206.9 4.4 %reshape.202 = bf16[64,2,8192]{2,1,0:T(2,128)(2,1)} reshape(bf16[128,8192]{1,0:T(8,128)(2,1)} %branch_0_fun.7) | data formatting | bytes 4194304 | tf_op jit(solution)/shard_map/cond/branch_0_fun/reshape | solution.py:380
  (28 shorter events, 0.3 us)
Async XLA Ops:
  6.7 88.1 %copy-start = (bf16[1,1088,1024]{2,1,0:T(8,128)(2,1)S(1)}, bf16[1,1088,1024]{2,1,0:T(8,128)(2,1)}, u32[]{:S(2)}) copy-start(bf16[1,1088,1024]{2,1,0:T(8,128)(2,1)} %param.12) | copy-start | bytes 6684676
  6.7 88.1 %copy-start.2 = (bf16[64,8192]{1,0:T(8,128)(2,1)S(1)}, bf16[64,8192]{1,0:T(8,128)(2,1)}, u32[]{:S(2)}) copy-start(bf16[64,8192]{1,0:T(8,128)(2,1)} %param.11) | copy-start | bytes 3145732
  6.7 88.1 %copy-start.4 = (s32[64,2]{0,1:T(2,128)S(1)}, s32[64,2]{0,1:T(2,128)}, u32[]{:S(2)}) copy-start(s32[64,2]{0,1:T(2,128)} %param.15) | copy-start | bytes 1540
  6.7 88.0 %all-to-all-start.4 = ((bf16[16,48,2048]{2,1,0:T(8,128)(2,1)}), bf16[16,48,2048]{2,1,0:T(8,128)(2,1)}, u32[]{:S(2)}, u32[]{:S(2)}) async-start(bf16[16,48,2048]{2,1,0:T(8,128)(2,1)} %bitcast.94), calls=%async_computation.4 | async-start | bytes 6291456 | tf_op jit(solution)/shard_map/all_to_all | solution.py:343
  110.7 41.3 %all-to-all-start.1 = ((bf16[16,48,1024]{2,1,0:T(8,128)(2,1)}), bf16[16,48,1024]{2,1,0:T(8,128)(2,1)}, u32[]{:S(2)}, u32[]{:S(2)}) async-start(bf16[16,48,1024]{2,1,0:T(8,128)(2,1)} %bitcast.98), calls=%async_computation.1 | async-start | bytes 3145728 | tf_op jit(solution)/shard_map/cond/branch_0_fun/all_to_all | solution.py:357
  151.9 41.3 %all-to-all-start = ((bf16[16,48,1024]{2,1,0:T(8,128)(2,1)}), bf16[16,48,1024]{2,1,0:T(8,128)(2,1)}, u32[]{:S(2)}, u32[]{:S(2)}) async-start(bf16[16,48,1024]{2,1,0:T(8,128)(2,1)} %bitcast.91), calls=%async_computation | async-start | bytes 3145728 | tf_op jit(solution)/shard_map/cond/branch_0_fun/all_to_all | solution.py:357

commit v4 on v3

--- a/solution.py
+++ b/solution.py
@@ -248,9 +248,10 @@
         peak = jnp.max(scores, axis=-1, keepdims=True)
         raised = jnp.exp2((scores - peak) * scale)
         mixed = jnp.dot(raised.astype(jnp.bfloat16), values, preferred_element_type=jnp.float32)
-        mixed = (mixed[:, :HEAD] / mixed[:, HEAD:]).astype(jnp.bfloat16)
-        out_ref[:, h * HEAD : (h + 1) * HEAD] = mixed[:rows]
-        out_ref[:, (h + 1) * HEAD : (h + 2) * HEAD] = mixed[rows:]
+        mixed = mixed[:, :HEAD] / mixed[:, HEAD:]
+        mixed = mixed.reshape(2 * tokens, per_token, HEAD).astype(jnp.bfloat16)
+        out_ref[:, :, h * HEAD : (h + 1) * HEAD] = mixed[:tokens]
+        out_ref[:, :, (h + 1) * HEAD : (h + 2) * HEAD] = mixed[tokens:]
 
 
 def attend_part(ret, pos, frozen_query, key_block, value_block, cached, per_token, cap, chunks,
@@ -280,8 +281,8 @@
         functools.partial(attend_kernel, per_token, heads, cap),
         grid=(folds,),
         in_specs=in_specs,
-        out_specs=pl.BlockSpec((rows, columns), place),
-        out_shape=jax.ShapeDtypeStruct((rows, model_width), jnp.bfloat16),
+        out_specs=pl.BlockSpec((tokens, per_token, columns), lambda g: (0, 0, g * chunks + chunk)),
+        out_shape=jax.ShapeDtypeStruct((tokens, per_token, model_width), jnp.bfloat16),
         scratch_shapes=[pltpu.VMEM((2 * rows, key_total), jnp.float32)],
         input_output_aliases=aliases,
         cost_estimate=pl.CostEstimate(
@@ -377,7 +378,7 @@
                 chunk,
                 context,
             )
-        return context.reshape(tokens, per_token, model_width)
+        return context
 
     if cap == most:
         return capped(arrived, lid, pos)

time: 212 us -> 208 us (0.981)
  local copies, waits for them, and re-layouts: 9.28 us -> 4.89 us
    reshape x1 -> x0, local copies, waits for them, and re-layouts: 4.38 us -> none  [capped(): return context.reshape(tokens, per_token, model_width)]
where the time goes in v4:
time: 208 us; the launch traced here: 207 us
  blocking collectives  79.1 us (38%)
  waiting for transfers between devices  53.3 us (26%)
  Pallas kernels  46.9 us (23%)
  starting transfers between devices  16.8 us (8%)
  local copies, waits for them, and re-layouts  4.89 us (2%)
  matrix products  2.75 us (1%)
  other arithmetic  2.51 us (1%)
    all_gather x1, blocking collectives, body(): lax.all_gather(adapter_index.reshape(1, rows), 'adapt', axis=0, tiled=True)  79.1 us
    all_to_all x2, waiting for transfers between devices, capped(): lax.all_to_all(delta.reshape(owners, block, width // chunks), 'adapt', sp...  53.3 us
    pallas_call x2, Pallas kernels, attend_part(): pl.pallas_call(functools.partial(attend_kernel, per_token, heads, cap), g...  27.6 us
    pallas_call x1, Pallas kernels, owner_part(): pl.pallas_call(functools.partial(owner_kernel, folds, cap, rank), grid=(f...  14.5 us
    all_to_all x2, starting transfers between devices, capped(): lax.all_to_all(delta.reshape(owners, block, width // chunks), 'adapt', sp...  9.95 us
    all_to_all x1, starting transfers between devices, body(): lax.all_to_all(outgoing.reshape(owners, block, width), 'adapt', split_axi...  6.82 us
    pallas_call x1, Pallas kernels, raise_part(): pl.pallas_call(functools.partial(raise_kernel, folds), grid=(tiles,), in_...  4.8 us
  transfers between devices with their start and end apart: 3, of which 2 were waited for; matrix products, arithmetic and copies ran while one was open for 1% of the time, Pallas kernels for 9%

profile of v4, /device:TPU:15, one launch (start us, length us, event | category | flops | bytes accessed | tf_op | source)
XLA Modules:
  0.0 207.1 jit_solution(3222982802033827291)
XLA Ops:
  0.0 0.8 copy.126
  0.8 0.7 broadcast_compare_fusion.2
  1.5 0.1 reshape.208
  1.6 0.2 convert_reduce_fusion.2
  1.8 0.1 reduce_sum.51
  2.0 0.1 copy.133
  2.1 0.2 slice_reduce_fusion.1
  2.3 0.1 eq.106
  2.4 0.1 eq.111
  2.5 1.3 fusion.111
  3.8 0.1 iota.93
  3.9 0.1 iota.100
  4.0 2.8 %convolution_convert_fusion.1 = bf16[768,2048]{1,0:T(8,128)(2,1)} fusion(bf16[64,2048]{1,0:T(8,128)(2,1)S(1)} %get-tuple-element.163, bf16[64,2048]{1,0:T(8,128)(2,1)S(1)} %get-tuple-element.161, bf16[64,2048]{1,0:T(8,128)(2,1)S(1)} %get-tuple-element.162, bf16[64,2048]{1,0:T(8,128)(2,1)S(1)} %get-tuple-element.160, s32[256]{0:T(256)S(1)} %iota.100, ...), kind=kOutput, calls=%fused_computation.56 | convolution fusion | flops 814022656 | bytes 4205312 | tf_op jit(solution)/shard_map/dot_general | solution.py:343
  6.7 6.8 %all-to-all-start.4 = ((bf16[16,48,2048]{2,1,0:T(8,128)(2,1)}), bf16[16,48,2048]{2,1,0:T(8,128)(2,1)}, u32[]{:S(2)}, u32[]{:S(2)}) async-start(bf16[16,48,2048]{2,1,0:T(8,128)(2,1)} %bitcast.94), calls=%async_computation.4 | async-start | bytes 6291456 | tf_op jit(solution)/shard_map/all_to_all | solution.py:344
  13.6 0.1 reshape.229
  13.7 79.1 %all-gather = s32[16,1,128]{2,1,0:T(1,128)S(1)} all-gather(s32[1,1,128]{2,1,0:T(1,128)S(1)} %reshape.229), channel_id=1, replica_groups=mesh['groups'=2,'adapt'=16] {'adapt'}, dimensions={0}, use_global_device_ids=true | all-gather | bytes 8704 | tf_op jit(solution)/shard_map/all_gather | solution.py:322
  92.8 0.3 convert_reduce_fusion.1
  93.2 0.6 reduce_max.18
  94.5 0.3 reduce_window_sum.11
  94.8 112.2 %conditional.1 = (bf16[64,2,8192]{2,1,0:T(2,128)(2,1)}) conditional(s32[]{:T(128)} %convert_element_type.55, (s32[128]{0:T(128)S(1)}, bf16[16,48,2048]{2,1,0:T(8,128)(2,1)}, bf16[8,32,8192]{2,1,0:T(8,128)(2,1)}, bf16[8,32,8192]{2,1,0:T(8,128)(2,1)}, pred[16,128]{1,0:T(8,128)(4,1)S(1)}, /*index=5*/bf16[1,1088,1024]{2,1,0:T(8,128)(2,1)S(1)}, ...), branch_computations={%region_5.6_spmd, %region_6.11_spmd} | conditional | flops 15837802496 | bytes 220158688 | solution.py:393
  94.9 0.3 select_reduce_fusion
  95.2 0.1 copy.114
  95.3 0.9 reshape.236.lid_ref
  96.2 14.5 %branch_0_fun.4 = (bf16[768,1024]{1,0:T(8,128)(2,1)}, bf16[768,1024]{1,0:T(8,128)(2,1)}) custom-call(s32[768,1]{1,0:T(8,128)} %reshape.236.lid_ref, bf16[768,2048]{1,0:T(8,128)(2,1)} %bitcast.1.rows_ref, bf16[256,8192]{1,0:T(8,128)(2,1)} %bitcast.93, bf16[256,8192]{1,0:T(8,128)(2,1)} %bitcast.77, bf16[256,8192]{1,0:T(8,128)(2,1)} %bitcast.78, ...), custom_call_target="tpu_custom_call" | custom-call | flops 9663676416 | bytes 40000000 | tf_op jit(solution)/shard_map/cond/branch_0_fun/pallas_call | solution.py:151
  110.6 5.0 %all-to-all-start.1 = ((bf16[16,48,1024]{2,1,0:T(8,128)(2,1)}), bf16[16,48,1024]{2,1,0:T(8,128)(2,1)}, u32[]{:S(2)}, u32[]{:S(2)}) async-start(bf16[16,48,1024]{2,1,0:T(8,128)(2,1)} %bitcast.98), calls=%async_computation.1 | async-start | bytes 3145728 | tf_op jit(solution)/shard_map/cond/branch_0_fun/all_to_all | solution.py:358
  115.6 4.8 %branch_0_fun.5 = bf16[768,1024]{1,0:T(8,128)(2,1)} custom-call(bf16[768,1024]{1,0:T(8,128)(2,1)} %get-tuple-element.48.blocked_ref, bf16[256,8192]{1,0:T(8,128)(2,1)} %bitcast.81, bf16[256,8192]{1,0:T(8,128)(2,1)} %bitcast.82, bf16[256,8192]{1,0:T(8,128)(2,1)} %bitcast.83, bf16[256,8192]{1,0:T(8,128)(2,1)} %bitcast.84), custom_call_target="tpu_custom_call" | custom-call | flops 1610612736 | bytes 12000000 | tf_op jit(solution)/shard_map/cond/branch_0_fun/pallas_call | solution.py:192
  120.4 31.5 %all-to-all-done.1 = bf16[16,48,1024]{2,1,0:T(8,128)(2,1)} async-done(((bf16[16,48,1024]{2,1,0:T(8,128)(2,1)}), bf16[16,48,1024]{2,1,0:T(8,128)(2,1)}, u32[]{:S(2)}, u32[]{:S(2)}) %all-to-all-start.1) | async-done | bytes 1572896 | tf_op jit(solution)/shard_map/cond/branch_0_fun/all_to_all | solution.py:358
  151.9 5.0 %all-to-all-start = ((bf16[16,48,1024]{2,1,0:T(8,128)(2,1)}), bf16[16,48,1024]{2,1,0:T(8,128)(2,1)}, u32[]{:S(2)}, u32[]{:S(2)}) async-start(bf16[16,48,1024]{2,1,0:T(8,128)(2,1)} %bitcast.91), calls=%async_computation | async-start | bytes 3145728 | tf_op jit(solution)/shard_map/cond/branch_0_fun/all_to_all | solution.py:358
  156.9 0.7 copy.117.pos_ref
  157.6 13.8 %branch_0_fun.6.rest_0_ = bf16[64,2,8192]{2,1,0:T(2,128)(2,1)} custom-call(s32[1]{0:T(128)} %get-tuple-element.42.cached_ref, s32[128,1]{1,0:T(8,128)} %copy.117.pos_ref, bf16[768,1024]{1,0:T(8,128)(2,1)} %bitcast.9.ret_ref, bf16[64,8192]{1,0:T(8,128)(2,1)S(1)} %get-tuple-element.49.frozen_ref, bf16[1088,1024]{1,0:T(8,128)(2,1)S(1)} %bitcast.85, ...), custom_call_target="tpu_custom_call" | custom-call | flops 2281701376 | bytes 40000000 | tf_op jit(solution)/shard_map/cond/branch_0_fun/pallas_call | solution.py:280
  171.4 21.8 %all-to-all-done = bf16[16,48,1024]{2,1,0:T(8,128)(2,1)} async-done(((bf16[16,48,1024]{2,1,0:T(8,128)(2,1)}), bf16[16,48,1024]{2,1,0:T(8,128)(2,1)}, u32[]{:S(2)}, u32[]{:S(2)}) %all-to-all-start) | async-done | bytes 1572896 | tf_op jit(solution)/shard_map/cond/branch_0_fun/all_to_all | solution.py:358
  193.2 13.8 %branch_0_fun.7 = bf16[64,2,8192]{2,1,0:T(2,128)(2,1)} custom-call(s32[1]{0:T(128)} %get-tuple-element.42.cached_ref, s32[128,1]{1,0:T(8,128)} %copy.117.pos_ref, bf16[768,1024]{1,0:T(8,128)(2,1)} %bitcast.5.ret_ref, bf16[64,8192]{1,0:T(8,128)(2,1)S(1)} %get-tuple-element.49.frozen_ref, ...), custom_call_target="tpu_custom_call", output_to_operand_aliasing={{}: (6, {})} | custom-call | flops 2281701376 | bytes 40000000 | tf_op jit(solution)/shard_map/cond/branch_0_fun/pallas_call | solution.py:280
  (27 shorter events, 0.2 us)
Async XLA Ops:
  6.7 88.1 %copy-start = (bf16[1,1088,1024]{2,1,0:T(8,128)(2,1)S(1)}, bf16[1,1088,1024]{2,1,0:T(8,128)(2,1)}, u32[]{:S(2)}) copy-start(bf16[1,1088,1024]{2,1,0:T(8,128)(2,1)} %param.12) | copy-start | bytes 6684676
  6.7 88.1 %copy-start.2 = (bf16[64,8192]{1,0:T(8,128)(2,1)S(1)}, bf16[64,8192]{1,0:T(8,128)(2,1)}, u32[]{:S(2)}) copy-start(bf16[64,8192]{1,0:T(8,128)(2,1)} %param.11) | copy-start | bytes 3145732
  6.7 88.1 %copy-start.4 = (s32[64,2]{0,1:T(2,128)S(1)}, s32[64,2]{0,1:T(2,128)}, u32[]{:S(2)}) copy-start(s32[64,2]{0,1:T(2,128)} %param.15) | copy-start | bytes 1540
  6.7 88.0 %all-to-all-start.4 = ((bf16[16,48,2048]{2,1,0:T(8,128)(2,1)}), bf16[16,48,2048]{2,1,0:T(8,128)(2,1)}, u32[]{:S(2)}, u32[]{:S(2)}) async-start(bf16[16,48,2048]{2,1,0:T(8,128)(2,1)} %bitcast.94), calls=%async_computation.4 | async-start | bytes 6291456 | tf_op jit(solution)/shard_map/all_to_all | solution.py:344
  110.6 41.3 %all-to-all-start.1 = ((bf16[16,48,1024]{2,1,0:T(8,128)(2,1)}), bf16[16,48,1024]{2,1,0:T(8,128)(2,1)}, u32[]{:S(2)}, u32[]{:S(2)}) async-start(bf16[16,48,1024]{2,1,0:T(8,128)(2,1)} %bitcast.98), calls=%async_computation.1 | async-start | bytes 3145728 | tf_op jit(solution)/shard_map/cond/branch_0_fun/all_to_all | solution.py:358
  151.9 41.3 %all-to-all-start = ((bf16[16,48,1024]{2,1,0:T(8,128)(2,1)}), bf16[16,48,1024]{2,1,0:T(8,128)(2,1)}, u32[]{:S(2)}, u32[]{:S(2)}) async-start(bf16[16,48,1024]{2,1,0:T(8,128)(2,1)} %bitcast.91), calls=%async_computation | async-start | bytes 3145728 | tf_op jit(solution)/shard_map/cond/branch_0_fun/all_to_all | solution.py:358
